TPU v7x, 32 devices: a whole 2x2x4 slice. The times are simulated.
32 devices in a mesh: node: 4 (over z), event: 8 (over y, x, core).
Axes of the slice: x: 2, y: 2, z: 4, core: 2. Of those that a mesh axis runs over, the one named last changes fastest.
Arguments:
- memory: bfloat16 [8192, 256], P('node'), may hold values from -6 to 6
- event_feat: bfloat16 [32, 32, 16, 128], P(('node', 'event')), may hold values from -6 to 6
- event_source: int32 [32, 32, 16], P(('node', 'event')), may hold values from 0 to 2047
- event_partner: int32 [32, 32, 16], P(('node', 'event')), may hold values from 0 to 511
- event_negative: int32 [32, 32, 16], P(('node', 'event')), may hold values from 0 to 511
- event_time: int32 [32, 32, 16], P(('node', 'event')), may hold values from 0 to 1023
- event_count: int32 [32, 32], P(('node', 'event')), may hold values from 0 to 16, as said below
- requests: int32 [32, 4, 128], P(('node', 'event')), may hold values from 0 to 2047
- w_input: bfloat16 [512, 768], replicated, may hold values from -0.25 to 0.25
- w_state: bfloat16 [256, 768], replicated, may hold values from -0.375 to 0.375
- w_pair: bfloat16 [256, 256], replicated, may hold values from -0.375 to 0.375
- gate_bias: float32 [768], replicated, may hold values from -3 to 3
- time_freq: float32 [128], replicated, may hold values from 0.001 to 1
Outputs:
- memory_grad: float32 [8192, 256], P(('node', 'event'))
Inputs may be any that keep to these rules, and one draw needn't show every extreme that they name: `event_count`: in every draw some device receives 16 live slots from every time block.
All inputs are finite; a program needn't handle non-finite values.
Results may differ from a plain program's by a relative error of at most 0.0021.
Values may be sent and summed in bfloat16 or wider, within the bound.
A program may use at most 64 MiB of HBM per device.

v0:
```python
import math

import jax
import jax.numpy as jnp
from jax import lax
from jax.sharding import PartitionSpec as P


def pair_grads(
    current, partner, negative, feature, timing, valid, w_input, w_state, w_pair, gate_bias
):
    width = current.shape[1]
    joined = jnp.concatenate([partner, feature, timing], axis=1)
    from_input = jnp.dot(joined, w_input, preferred_element_type=jnp.float32)
    from_state = jnp.dot(current, w_state, preferred_element_type=jnp.float32)
    reset = jax.nn.sigmoid(from_input[:, :width] + from_state[:, :width] + gate_bias[:width])
    update = jax.nn.sigmoid(
        from_input[:, width : 2 * width]
        + from_state[:, width : 2 * width]
        + gate_bias[width : 2 * width]
    )
    recurrent = from_state[:, 2 * width :]
    candidate = jnp.tanh(from_input[:, 2 * width :] + gate_bias[2 * width :] + reset * recurrent)
    previous = current.astype(jnp.float32)
    renewed = (1.0 - update) * candidate + update * previous
    factor = 1.0 / math.sqrt(width)
    key_pos = jnp.dot(partner, w_pair, preferred_element_type=jnp.float32)
    key_neg = jnp.dot(negative, w_pair, preferred_element_type=jnp.float32)
    score_pos = jnp.sum(renewed * key_pos, axis=1) * factor
    score_neg = jnp.sum(renewed * key_neg, axis=1) * factor
    weight_pos = -valid * jax.nn.sigmoid(-score_pos)
    weight_neg = valid * jax.nn.sigmoid(score_neg)
    grad_renewed = (weight_pos[:, None] * key_pos + weight_neg[:, None] * key_neg) * factor
    grad_keypos = (weight_pos[:, None] * renewed * factor).astype(jnp.bfloat16)
    grad_keyneg = (weight_neg[:, None] * renewed * factor).astype(jnp.bfloat16)
    grad_cand = grad_renewed * (1.0 - update) * (1.0 - candidate * candidate)
    grad_reset = grad_cand * recurrent * reset * (1.0 - reset)
    grad_update = grad_renewed * (previous - candidate) * update * (1.0 - update)
    input_back = jnp.concatenate([grad_reset, grad_update, grad_cand], axis=1).astype(jnp.bfloat16)
    state_back = jnp.concatenate([grad_reset, grad_update, grad_cand * reset], axis=1).astype(
        jnp.bfloat16
    )
    through_input = jnp.dot(input_back, w_input.T, preferred_element_type=jnp.float32)
    grad_current = grad_renewed * update + jnp.dot(
        state_back, w_state.T, preferred_element_type=jnp.float32
    )
    grad_partner = through_input[:, :width] + jnp.dot(
        grad_keypos, w_pair.T, preferred_element_type=jnp.float32
    )
    grad_negative = jnp.dot(grad_keyneg, w_pair.T, preferred_element_type=jnp.float32)
    return (grad_current, grad_partner, grad_negative)


def pick_rows(values, row_ids):
    selector = (row_ids[:, None] == jnp.arange(values.shape[0], dtype=jnp.int32)[None, :]).astype(
        values.dtype
    )
    return jnp.dot(selector, values, preferred_element_type=jnp.float32).astype(values.dtype)


def add_rows(total, row_ids, grads):
    selector = (row_ids[:, None] == jnp.arange(total.shape[0], dtype=jnp.int32)[None, :]).astype(
        jnp.float32
    )
    summed = lax.dot_general(
        selector,
        grads,
        (((0,), (0,)), ((), ())),
        precision=lax.Precision.HIGHEST,
        preferred_element_type=jnp.float32,
    )
    return total + summed


def local(
    memory,
    event_feat,
    event_source,
    event_partner,
    event_negative,
    event_time,
    event_count,
    requests,
    w_input,
    w_state,
    w_pair,
    gate_bias,
    time_freq,
):
    node_total = lax.axis_size("node")
    event_total = lax.axis_size("event")
    shards = node_total * event_total
    slots_cap = event_feat.shape[2]
    feat_width = event_feat.shape[3]
    width = memory.shape[1]
    group_rows = memory.shape[0]
    arrived = (
        lax.all_to_all(event_feat, ("node", "event"), split_axis=1, concat_axis=0, tiled=True),
        lax.all_to_all(event_source, ("node", "event"), split_axis=1, concat_axis=0, tiled=True),
        lax.all_to_all(event_partner, ("node", "event"), split_axis=1, concat_axis=0, tiled=True),
        lax.all_to_all(event_negative, ("node", "event"), split_axis=1, concat_axis=0, tiled=True),
        lax.all_to_all(event_time, ("node", "event"), split_axis=1, concat_axis=0, tiled=True),
        lax.all_to_all(event_count, ("node", "event"), split_axis=1, concat_axis=0, tiled=True),
    )
    incoming = lax.all_to_all(requests, "node", split_axis=1, concat_axis=1, tiled=True)
    wanted = incoming.reshape(-1)
    fetched = pick_rows(memory, wanted).reshape(incoming.shape + (width,))
    table = lax.all_to_all(fetched, "node", split_axis=1, concat_axis=1, tiled=True).reshape(
        -1, width
    )
    total_rows = shards * slots_cap
    block_rows = math.gcd(total_rows, 1024)
    turns = total_rows // block_rows
    column = jnp.arange(slots_cap, dtype=jnp.int32)
    valid_all = (column[None, :] < arrived[5]).astype(jnp.float32)
    features = arrived[0].reshape(turns, block_rows, feat_width)
    sources = arrived[1].reshape(turns, block_rows)
    partners = arrived[2].reshape(turns, block_rows)
    negatives = arrived[3].reshape(turns, block_rows)
    timings = arrived[4].reshape(turns, block_rows)
    valids = valid_all.reshape(turns, block_rows)

    def one_block(carry, pieces):
        state_grad, table_grad = carry
        feature, source_ids, partner_ids, negative_ids, time_bins, valid = pieces
        timing = jnp.cos(time_bins.astype(jnp.float32)[:, None] * time_freq[None, :]).astype(
            jnp.bfloat16
        )
        grad_current, grad_partner, grad_negative = pair_grads(
            pick_rows(memory, source_ids),
            pick_rows(table, partner_ids),
            pick_rows(table, negative_ids),
            feature,
            timing,
            valid,
            w_input,
            w_state,
            w_pair,
            gate_bias,
        )
        state_grad = add_rows(state_grad, source_ids, grad_current)
        table_grad = add_rows(
            add_rows(table_grad, partner_ids, grad_partner), negative_ids, grad_negative
        )
        return ((state_grad, table_grad), None)

    start_carry = (
        jnp.zeros((group_rows, width), jnp.float32),
        jnp.zeros((table.shape[0], width), jnp.float32),
    )
    (state_grad, table_grad), _ = lax.scan(
        one_block, start_carry, (features, sources, partners, negatives, timings, valids)
    )
    returned = lax.all_to_all(
        table_grad.reshape(incoming.shape + (width,)),
        "node",
        split_axis=1,
        concat_axis=1,
        tiled=True,
    )
    state_grad = add_rows(state_grad, wanted, returned.reshape(-1, width))
    return lax.psum_scatter(state_grad, "event", scatter_dimension=0, tiled=True)


def solution(mesh):
    in_specs = (
        P("node", None),
        P(("node", "event"), None, None, None),
        P(("node", "event"), None, None),
        P(("node", "event"), None, None),
        P(("node", "event"), None, None),
        P(("node", "event"), None, None),
        P(("node", "event"), None),
        P(("node", "event"), None, None),
        P(),
        P(),
        P(),
        P(),
        P(),
    )
    out_specs = P(("node", "event"), None)
    return jax.shard_map(local, mesh=mesh, in_specs=in_specs, out_specs=out_specs, check_vma=False)
```

profile of v0, /device:TPU:0, one launch (start us, length us, event | category | flops | bytes accessed | tf_op | source)
XLA Modules:
  0.0 184.5 jit_solution(14549111810283862196)
XLA Ops:
  6.5 0.8 copy.46
  7.4 14.2 %all_to_all.73 = s32[1,32,1]{2,0,1:T(1,128)S(1)} all-to-all(s32[1,32,1]{2,0,1:T(1,128)S(1)} %copy.46), channel_id=1, replica_groups=mesh['node'=4,'event'=8] {'node','event'}, dimensions={1} | all-to-all | bytes 256 | tf_op jit(solution)/shard_map/all_to_all | solution.py:103
  21.6 3.2 %all-to-all-start.3 = ((s32[1,4,128]{2,0,1:T(1,128)}), s32[1,4,128]{2,0,1:T(1,128)S(1)}, u32[]{:S(2)}, u32[]{:S(2)}) async-start(s32[1,4,128]{2,0,1:T(1,128)} %bitcast.35), calls=%async_computation.3 | async-start | bytes 4096 | tf_op jit(solution)/shard_map/all_to_all | solution.py:105
  24.8 1.4 copy.47
  26.2 4.1 %all-to-all-done.3 = s32[1,4,128]{2,0,1:T(1,128)S(1)} async-done(((s32[1,4,128]{2,0,1:T(1,128)}), s32[1,4,128]{2,0,1:T(1,128)S(1)}, u32[]{:S(2)}, u32[]{:S(2)}) %all-to-all-start.3) | async-done | bytes 2080 | tf_op jit(solution)/shard_map/all_to_all | solution.py:105
  30.3 2.5 %all-to-all-start.2 = ((s32[1,32,16]{2,0,1:T(1,128)}), s32[1,32,16]{2,0,1:T(1,128)S(1)}, u32[]{:S(2)}, u32[]{:S(2)}) async-start(s32[1,32,16]{2,0,1:T(1,128)} %copy.47), calls=%async_computation.2 | async-start | bytes 32768 | tf_op jit(solution)/shard_map/all_to_all | solution.py:100
  32.8 1.4 fusion.61
  34.2 1.4 copy.51
  35.6 1.4 copy.45
  37.0 1.4 copy.56
  38.3 0.7 reduce.1
  39.0 0.9 all-to-all-done.2
  39.9 4.9 %all-to-all-start.6 = ((s32[1,32,16]{2,0,1:T(1,128)}), s32[1,32,16]{2,0,1:T(1,128)S(1)}, u32[]{:S(2)}, u32[]{:S(2)}) async-start(s32[1,32,16]{2,0,1:T(1,128)} %copy.51), calls=%async_computation.6 | async-start | bytes 32768 | tf_op jit(solution)/shard_map/all_to_all | solution.py:102
  44.9 0.7 lt.31
  45.6 6.4 %all-to-all-done.6 = s32[1,32,16]{2,0,1:T(1,128)S(1)} async-done(((s32[1,32,16]{2,0,1:T(1,128)}), s32[1,32,16]{2,0,1:T(1,128)S(1)}, u32[]{:S(2)}, u32[]{:S(2)}) %all-to-all-start.6) | async-done | bytes 2080 | tf_op jit(solution)/shard_map/all_to_all | solution.py:102
  52.0 2.5 %all-to-all-start = ((s32[1,32,16]{2,0,1:T(1,128)}), s32[1,32,16]{2,0,1:T(1,128)S(1)}, u32[]{:S(2)}, u32[]{:S(2)}) async-start(s32[1,32,16]{2,0,1:T(1,128)} %copy.45), calls=%async_computation | async-start | bytes 32768 | tf_op jit(solution)/shard_map/all_to_all | solution.py:99
  54.5 1.6 fusion.10
  56.1 5.6 %all-to-all-done = s32[1,32,16]{2,0,1:T(1,128)S(1)} async-done(((s32[1,32,16]{2,0,1:T(1,128)}), s32[1,32,16]{2,0,1:T(1,128)S(1)}, u32[]{:S(2)}, u32[]{:S(2)}) %all-to-all-start) | async-done | bytes 2080 | tf_op jit(solution)/shard_map/all_to_all | solution.py:99
  61.6 2.6 %all-to-all-start.7 = ((s32[1,32,16]{2,0,1:T(1,128)}), s32[1,32,16]{2,0,1:T(1,128)S(1)}, u32[]{:S(2)}, u32[]{:S(2)}) async-start(s32[1,32,16]{2,0,1:T(1,128)} %copy.56), calls=%async_computation.7 | async-start | bytes 32768 | tf_op jit(solution)/shard_map/all_to_all | solution.py:101
  64.3 0.5 broadcast.90
  64.9 0.6 reduce.14
  65.5 5.8 %all-to-all-done.7 = s32[1,32,16]{2,0,1:T(1,128)S(1)} async-done(((s32[1,32,16]{2,0,1:T(1,128)}), s32[1,32,16]{2,0,1:T(1,128)S(1)}, u32[]{:S(2)}, u32[]{:S(2)}) %all-to-all-start.7) | async-done | bytes 2080 | tf_op jit(solution)/shard_map/all_to_all | solution.py:101
  71.3 2.6 %all-to-all-start.5 = ((bf16[1,32,16,128]{3,2,0,1:T(8,128)(2,1)}), bf16[1,32,16,128]{3,2,0,1:T(8,128)(2,1)S(1)}, u32[]{:S(2)}, u32[]{:S(2)}) async-start(bf16[1,32,16,128]{3,2,0,1:T(8,128)(2,1)} %bitcast.6), calls=%async_computation.5 | async-start | bytes 262144 | tf_op jit(solution)/shard_map/all_to_all | solution.py:98
  74.0 0.9 fusion.9
  74.8 7.3 %all-to-all-done.5 = bf16[1,32,16,128]{3,2,0,1:T(8,128)(2,1)S(1)} async-done(((bf16[1,32,16,128]{3,2,0,1:T(8,128)(2,1)}), bf16[1,32,16,128]{3,2,0,1:T(8,128)(2,1)S(1)}, u32[]{:S(2)}, u32[]{:S(2)}) %all-to-all-start.5) | async-done | bytes 131104 | tf_op jit(solution)/shard_map/all_to_all | solution.py:98
  82.2 4.0 %all-to-all-start.4 = ((bf16[1,4,128,256]{3,2,0,1:T(8,128)(2,1)}), bf16[1,4,128,256]{3,2,0,1:T(8,128)(2,1)}, u32[]{:S(2)}, u32[]{:S(2)}) async-start(bf16[1,4,128,256]{3,2,0,1:T(8,128)(2,1)} %bitcast.4), calls=%async_computation.4 | async-start | bytes 524288 | tf_op jit(solution)/shard_map/all_to_all | solution.py:108
  86.2 1.6 cosine_convert_fusion
  87.8 0.6 reduce.15
  88.5 0.6 reduce.16
  89.6 0.8 copy.52
  90.3 5.5 %all-to-all-done.4 = bf16[1,4,128,256]{3,2,0,1:T(8,128)(2,1)} async-done(((bf16[1,4,128,256]{3,2,0,1:T(8,128)(2,1)}), bf16[1,4,128,256]{3,2,0,1:T(8,128)(2,1)}, u32[]{:S(2)}, u32[]{:S(2)}) %all-to-all-start.4) | async-done | bytes 262176 | tf_op jit(solution)/shard_map/all_to_all | solution.py:108
  95.8 1.5 convolution_convert_fusion.1
  97.6 2.7 %fusion.34 = f32[512,768]{1,0:T(8,128)} fusion(bf16[512,768]{1,0:T(8,128)(2,1)S(1)} %copy-done.17, bf16[512,128]{0,1:T(8,128)(2,1)} %cosine_convert_fusion, bf16[512,128]{0,1:T(8,128)(2,1)S(1)} %copy-done.13, bf16[512,256]{0,1:T(8,128)(2,1)S(1)} %convolution_convert_fusion.1), kind=kOutput, calls=%fused_computation.49 | convolution fusion | flops 404226048 | bytes 2883584 | tf_op jit(solution)/shard_map/while/body/eval_jaxpr/dot_general | solution.py:14
  100.3 4.2 %multiply_reduce_fusion = (f32[512]{0:T(512)S(1)}, f32[512]{0:T(512)}, f32[512,256]{1,0:T(8,128)}, f32[512,256]{1,0:T(8,128)}, f32[512,256]{1,0:T(8,128)}, /*index=5*/f32[512,256]{1,0:T(8,128)}, f32[512,256]{1,0:T(8,128)}) fusion(f32[512,256]{1,0:T(8,128)S(1)} %fusion.63, bf16[512,256]{1,0:T(8,128)(2,1)S(1)} %fusion.9, f32[512,768]{1,0:T(8,128)S(1)} %fusion.62, ...), kind=kOutput, calls=%fused_computation.61 | convolution fusion | flops 204602368 | bytes 6956032 | tf_op jit(solution)/shard_map/while/body/eval_jaxpr/dot_general | solution.py:28
  104.6 0.8 divide_select_fusion
  105.4 1.3 fusion.47
  106.7 1.3 fusion.46
  108.1 1.0 multiply_convert_fusion.2
  109.4 0.5 copy-done.3
  109.9 0.5 copy-done.18
  110.8 1.1 fusion.12
  112.0 1.9 %convolution_add_fusion.2 = f32[512,256]{1,0:T(8,128)} fusion(f32[512,256]{1,0:T(8,128)S(1)} %fusion.12, f32[512,256]{1,0:T(8,128)S(1)} %fusion.47, s32[512]{0:T(512)S(1)} %eq.118), kind=kOutput, calls=%fused_computation.13 | convolution fusion | flops 805699584 | bytes 1574912 | tf_op jit(solution)/shard_map/while/body/eval_jaxpr/dot_general | solution.py:65
  113.9 3.5 %all-to-all-start.8 = ((f32[1,4,128,256]{3,2,0,1:T(8,128)}), f32[1,4,128,256]{3,2,0,1:T(8,128)S(1)}, u32[]{:S(2)}, u32[]{:S(2)}) async-start(f32[1,4,128,256]{3,2,0,1:T(8,128)} %bitcast.9), calls=%async_computation.8 | async-start | bytes 1048576 | tf_op jit(solution)/shard_map/all_to_all | solution.py:154
  117.6 1.5 convolution_add_fusion.1
  119.2 11.3 %all-to-all-done.8 = f32[1,4,128,256]{3,2,0,1:T(8,128)S(1)} async-done(((f32[1,4,128,256]{3,2,0,1:T(8,128)}), f32[1,4,128,256]{3,2,0,1:T(8,128)S(1)}, u32[]{:S(2)}, u32[]{:S(2)}) %all-to-all-start.8) | async-done | bytes 524320 | tf_op jit(solution)/shard_map/all_to_all | solution.py:154
  130.5 3.6 %fusion = f32[2048,256]{1,0:T(8,128)S(1)} fusion(f32[512,256]{1,0:T(8,128)S(1)} %bitcast.33, s32[512]{0:T(512)S(1)} %bitcast.37), kind=kOutput, calls=%fused_computation.1 | convolution fusion | flops 3222274048 | bytes 2623488 | tf_op jit(solution)/shard_map/dot_general | solution.py:65
  134.1 4.9 %fusion.4 = f32[2048,256]{1,0:T(8,128)} fusion(f32[2048,256]{1,0:T(8,128)S(1)} %fusion, f32[512,256]{1,0:T(8,128)S(1)} %convolution_add_fusion.1, s32[512]{0:T(512)S(1)} %eq.92), kind=kOutput, calls=%fused_computation.6 | convolution fusion | flops 3222798336 | bytes 4720640 | tf_op jit(solution)/shard_map/while/body/eval_jaxpr/dot_general | solution.py:65
  139.1 38.6 %reduce-scatter.2.cloned.1.call-done = f32[256,256]{1,0:T(8,128)} async-done(((f32[2048,256]{1,0:T(8,128)}), f32[256,256]{1,0:T(8,128)}) %reduce-scatter.2.cloned.1.call-update) | async-done | bytes 262160 | tf_op jit(solution)/shard_map/reduce_scatter | solution.py:162
  (48 shorter events, 2.1 us)
Async XLA Ops:
  6.5 48.0 %copy-start = (bf16[2048,256]{1,0:T(8,128)(2,1)S(1)}, bf16[2048,256]{1,0:T(8,128)(2,1)}, u32[]{:S(2)}) copy-start(bf16[2048,256]{1,0:T(8,128)(2,1)} %param.13) | copy-start | bytes 3145732
  21.6 8.7 %all-to-all-start.3 = ((s32[1,4,128]{2,0,1:T(1,128)}), s32[1,4,128]{2,0,1:T(1,128)S(1)}, u32[]{:S(2)}, u32[]{:S(2)}) async-start(s32[1,4,128]{2,0,1:T(1,128)} %bitcast.35), calls=%async_computation.3 | async-start | bytes 4096 | tf_op jit(solution)/shard_map/all_to_all | solution.py:105
  30.3 25.8 %copy-start.14 = (s32[1,4,128]{2,0,1:T(1,128)}, s32[1,4,128]{2,0,1:T(1,128)S(1)}, u32[]{:S(2)}) copy-start(s32[1,4,128]{2,0,1:T(1,128)S(1)} %all-to-all-done.3) | copy-start | bytes 6148
  30.3 9.6 %all-to-all-start.2 = ((s32[1,32,16]{2,0,1:T(1,128)}), s32[1,32,16]{2,0,1:T(1,128)S(1)}, u32[]{:S(2)}, u32[]{:S(2)}) async-start(s32[1,32,16]{2,0,1:T(1,128)} %copy.47), calls=%async_computation.2 | async-start | bytes 32768 | tf_op jit(solution)/shard_map/all_to_all | solution.py:100
  39.9 12.1 %all-to-all-start.6 = ((s32[1,32,16]{2,0,1:T(1,128)}), s32[1,32,16]{2,0,1:T(1,128)S(1)}, u32[]{:S(2)}, u32[]{:S(2)}) async-start(s32[1,32,16]{2,0,1:T(1,128)} %copy.51), calls=%async_computation.6 | async-start | bytes 32768 | tf_op jit(solution)/shard_map/all_to_all | solution.py:102
  52.0 9.6 %all-to-all-start = ((s32[1,32,16]{2,0,1:T(1,128)}), s32[1,32,16]{2,0,1:T(1,128)S(1)}, u32[]{:S(2)}, u32[]{:S(2)}) async-start(s32[1,32,16]{2,0,1:T(1,128)} %copy.45), calls=%async_computation | async-start | bytes 32768 | tf_op jit(solution)/shard_map/all_to_all | solution.py:99
  61.6 9.7 %all-to-all-start.7 = ((s32[1,32,16]{2,0,1:T(1,128)}), s32[1,32,16]{2,0,1:T(1,128)S(1)}, u32[]{:S(2)}, u32[]{:S(2)}) async-start(s32[1,32,16]{2,0,1:T(1,128)} %copy.56), calls=%async_computation.7 | async-start | bytes 32768 | tf_op jit(solution)/shard_map/all_to_all | solution.py:101
  71.3 10.8 %all-to-all-start.5 = ((bf16[1,32,16,128]{3,2,0,1:T(8,128)(2,1)}), bf16[1,32,16,128]{3,2,0,1:T(8,128)(2,1)S(1)}, u32[]{:S(2)}, u32[]{:S(2)}) async-start(bf16[1,32,16,128]{3,2,0,1:T(8,128)(2,1)} %bitcast.6), calls=%async_computation.5 | async-start | bytes 262144 | tf_op jit(solution)/shard_map/all_to_all | solution.py:98
  73.9 12.3 %copy-start.16 = (f32[128]{0:T(128)S(1)}, f32[128]{0:T(128)}, u32[]{:S(2)}) copy-start(f32[128]{0:T(128)} %param.25) | copy-start | bytes 1540
  73.9 15.2 %copy-start.9 = (bf16[256,768]{1,0:T(8,128)(2,1)S(1)}, bf16[256,768]{1,0:T(8,128)(2,1)}, u32[]{:S(2)}) copy-start(bf16[256,768]{1,0:T(8,128)(2,1)} %param.22) | copy-start | bytes 1179652
  82.2 13.6 %all-to-all-start.4 = ((bf16[1,4,128,256]{3,2,0,1:T(8,128)(2,1)}), bf16[1,4,128,256]{3,2,0,1:T(8,128)(2,1)}, u32[]{:S(2)}, u32[]{:S(2)}) async-start(bf16[1,4,128,256]{3,2,0,1:T(8,128)(2,1)} %bitcast.4), calls=%async_computation.4 | async-start | bytes 524288 | tf_op jit(solution)/shard_map/all_to_all | solution.py:108
  89.2 8.2 %copy-start.7 = (bf16[256,256]{1,0:T(8,128)(2,1)S(1)}, bf16[256,256]{1,0:T(8,128)(2,1)}, u32[]{:S(2)}) copy-start(bf16[256,256]{1,0:T(8,128)(2,1)} %param.23) | copy-start | bytes 393220
  95.8 1.8 copy-start.13
  95.8 1.8 copy-start.17
  104.5 3.5 %copy-start.1 = (f32[512,256]{1,0:T(8,128)S(1)}, f32[512,256]{1,0:T(8,128)}, u32[]{:S(2)}) copy-start(f32[512,256]{1,0:T(8,128)} %get-tuple-element.43) | copy-start | bytes 1572868
  104.6 3.5 %copy-start.5 = (f32[512,256]{1,0:T(8,128)S(1)}, f32[512,256]{1,0:T(8,128)}, u32[]{:S(2)}) copy-start(f32[512,256]{1,0:T(8,128)} %get-tuple-element.41) | copy-start | bytes 1572868
  104.6 3.5 %copy-start.6 = (f32[512,256]{1,0:T(8,128)S(1)}, f32[512,256]{1,0:T(8,128)}, u32[]{:S(2)}) copy-start(f32[512,256]{1,0:T(8,128)} %get-tuple-element.42) | copy-start | bytes 1572868
  104.6 3.5 %copy-start.8 = (f32[512,256]{1,0:T(8,128)S(1)}, f32[512,256]{1,0:T(8,128)}, u32[]{:S(2)}) copy-start(f32[512,256]{1,0:T(8,128)} %get-tuple-element.69) | copy-start | bytes 1572868
  109.1 0.8 copy-start.3
  109.1 1.3 copy-start.18
  109.9 0.9 copy-start.11
  109.9 0.9 copy-start.12
  111.9 5.7 %copy-start.2 = (f32[512,256]{1,0:T(8,128)S(1)}, f32[512,256]{1,0:T(8,128)}, u32[]{:S(2)}) copy-start(f32[512,256]{1,0:T(8,128)} %get-tuple-element.43) | copy-start | bytes 1572868
  112.0 5.7 %copy-start.4 = (f32[512,256]{1,0:T(8,128)S(1)}, f32[512,256]{1,0:T(8,128)}, u32[]{:S(2)}) copy-start(f32[512,256]{1,0:T(8,128)} %copy-done.3) | copy-start | bytes 1572868
  112.0 5.7 %copy-start.10 = (bf16[256,768]{1,0:T(8,128)(2,1)S(1)}, bf16[256,768]{1,0:T(8,128)(2,1)}, u32[]{:S(2)}) copy-start(bf16[256,768]{1,0:T(8,128)(2,1)} %param.22) | copy-start | bytes 1179652
  113.9 16.6 %all-to-all-start.8 = ((f32[1,4,128,256]{3,2,0,1:T(8,128)}), f32[1,4,128,256]{3,2,0,1:T(8,128)S(1)}, u32[]{:S(2)}, u32[]{:S(2)}) async-start(f32[1,4,128,256]{3,2,0,1:T(8,128)} %bitcast.9), calls=%async_computation.8 | async-start | bytes 1048576 | tf_op jit(solution)/shard_map/all_to_all | solution.py:154
  117.4 13.1 %copy-start.15 = (s32[1,4,128]{2,0,1:T(1,128)S(1)}, s32[1,4,128]{2,0,1:T(1,128)}, u32[]{:S(2)}) copy-start(s32[1,4,128]{2,0,1:T(1,128)} %copy-done.14) | copy-start | bytes 6148
  117.4 60.3 %reduce-scatter.2.cloned.1.call-start = ((), (), s32[]{:S(2)}) async-start(), calls=%async_computation.10 | async-start | bytes 2359296 | tf_op jit(solution)/shard_map/reduce_scatter | solution.py:162
Sparse Core Ops, SparseCore 0:
  139.2 38.4 reduce-scatter.1
where the time goes:
time: 185 us; the launch traced here: 184 us
  waiting for transfers between devices  85.5 us (46%)
  matrix products  27.6 us (15%)
  starting transfers between devices  26.1 us (14%)
  blocking collectives  14.2 us (8%)
  between operations  13.7 us (7%)
  local copies, waits for them, and re-layouts  11.1 us (6%)
  other arithmetic  6.27 us (3%)
    reduce_scatter x1, waiting for transfers between devices, local(): lax.psum_scatter(state_grad, 'event', scatter_dimension=0, tiled=True)  38.6 us
    all_to_all x1, blocking collectives, local(): lax.all_to_all(event_count, ('node', 'event'), split_axis=1, concat_axis=...  14.2 us
    dot_general x4, matrix products, add_rows(): lax.dot_general(selector, grads, (((0,), (0,)), ((), ())), precision=lax....  11.6 us
    all_to_all x1, waiting for transfers between devices, local(): lax.all_to_all(table_grad.reshape(incoming.shape + (width,)), 'node', spl...  11.3 us
    all_to_all x1, waiting for transfers between devices, local(): lax.all_to_all(event_feat, ('node', 'event'), split_axis=1, concat_axis=0...  7.33 us
    unnamed x42, local copies, waits for them, and re-layouts  6.59 us
    all_to_all x1, waiting for transfers between devices, local(): lax.all_to_all(event_time, ('node', 'event'), split_axis=1, concat_axis=0...  6.4 us
    all_to_all x1, waiting for transfers between devices, local(): lax.all_to_all(event_negative, ('node', 'event'), split_axis=1, concat_ax...  5.81 us
  transfers between devices with their start and end apart: 9, of which 9 were waited for; matrix products, arithmetic and copies ran while one was open for 10% of the time, Pallas kernels for 0%

commit v1 on v0

v1 whole, which is shorter than its diff:
```python
import functools
import math

import jax
import jax.numpy as jnp
from jax import lax
from jax.experimental import pallas as pl
from jax.experimental.pallas import tpu as pltpu
from jax.sharding import PartitionSpec as P

MESH = pl.DeviceIdType.MESH
BF = jnp.bfloat16
F32 = jnp.float32
LANES = 128


def mm(a, b):
    return jnp.dot(a, b, preferred_element_type=F32)


def mm_nt(a, b):
    return lax.dot_general(a, b, (((1,), (1,)), ((), ())), preferred_element_type=F32)


def split(value):
    high = value.astype(BF)
    return high, (value - high.astype(F32)).astype(BF)


def one_hot(mask):
    return jnp.where(mask, 1.0, 0.0).astype(BF)


def pick_matrix(column, total):
    lane = lax.broadcasted_iota(jnp.int32, column.shape, 1)
    return jnp.concatenate(
        [one_hot(column == lane + start) for start in range(0, total, LANES)], axis=1
    )


def spread_matrix(row, total, base):
    ids = lax.broadcasted_iota(jnp.int32, (total, row.shape[1]), 0) + base
    return one_hot(ids == row)


def kernel(
    n_node,
    n_event,
    chunk,
    pack_ref,
    feat_ref,
    req_ref,
    mem_hbm,
    win_hbm,
    wst_hbm,
    wpair_hbm,
    bias_ref,
    freq_ref,
    out_ref,
    mem,
    win,
    wst,
    wpair,
    feats,
    packs,
    wanted,
    fetched,
    table,
    pre,
    recur,
    prev,
    ids_row,
    ids_col,
    table_grad,
    cur_high,
    cur_low,
    back_out,
    back_in,
    own_low,
    acc,
    pair_out,
    pair_in,
    block_out,
    block_in,
    load_sem,
    feat_send,
    feat_recv,
    pack_send,
    pack_recv,
    req_send,
    req_recv,
    tab_send,
    tab_recv,
    back_send,
    back_recv,
    pair_send,
    pair_recv,
    block_send,
    block_recv,
):
    shards = n_node * n_event
    node, event = lax.axis_index("node"), lax.axis_index("event")
    me = node * n_event + event
    slots = feat_ref.shape[1]
    width = mem.shape[1]
    group_rows = mem.shape[0]
    asked = req_ref.shape[2]
    table_rows = n_node * asked
    events = shards * slots
    turns = events // chunk
    chips = n_event // 2
    chip, core = event // 2, event % 2
    sibling = event + 1 - 2 * core
    block = group_rows // n_event

    barrier = pltpu.get_barrier_semaphore()

    @pl.loop(1, shards)
    def _(k):
        peer = lax.rem(me + k, shards)
        pl.semaphore_signal(
            barrier, inc=1, device_id=(peer // n_event, peer % n_event), device_id_type=MESH
        )

    loads = [
        pltpu.make_async_copy(mem_hbm, mem, load_sem.at[0]),
        pltpu.make_async_copy(win_hbm, win, load_sem.at[1]),
        pltpu.make_async_copy(wst_hbm, wst, load_sem.at[2]),
        pltpu.make_async_copy(wpair_hbm, wpair, load_sem.at[3]),
    ]
    for load in loads:
        load.start()
    own_feat = pltpu.make_async_copy(feat_ref.at[me], feats.at[me], feat_recv)
    own_feat.start()
    packs[me] = pack_ref[me]
    wanted[node] = req_ref[node]
    pl.semaphore_wait(barrier, shards - 1)

    def to_node(k):
        return lax.rem(node + k, n_node)

    def request_copy(k):
        peer = to_node(k)
        return pltpu.make_async_remote_copy(
            src_ref=req_ref.at[peer],
            dst_ref=wanted.at[node],
            send_sem=req_send.at[peer],
            recv_sem=req_recv.at[node],
            device_id=(peer, event),
            device_id_type=MESH,
        )

    for k in range(1, n_node):
        request_copy(k).start()

    @pl.loop(1, shards)
    def _(k):
        peer = lax.rem(me + k, shards)
        target = (peer // n_event, peer % n_event)
        pltpu.make_async_remote_copy(
            src_ref=pack_ref.at[peer],
            dst_ref=packs.at[me],
            send_sem=pack_send,
            recv_sem=pack_recv,
            device_id=target,
            device_id_type=MESH,
        ).start()
        pltpu.make_async_remote_copy(
            src_ref=feat_ref.at[peer],
            dst_ref=feats.at[me],
            send_sem=feat_send,
            recv_sem=feat_recv,
            device_id=target,
            device_id_type=MESH,
        ).start()

    def arrived(buffer, sem, slot):
        pltpu.make_async_copy(buffer.at[slot], buffer.at[slot], sem.at[slot]).wait()

    for k in range(1, n_node):
        arrived(wanted, req_recv, to_node(k))
    loads[0].wait()
    rows = []
    for g in range(n_node):
        spread = jnp.broadcast_to(wanted[g], (LANES, asked))
        rows.append(spread.T)
    picked = mm(pick_matrix(jnp.concatenate(rows, axis=0), group_rows), mem[...]).astype(BF)
    fetched[...] = picked.reshape(n_node, asked, width)

    def table_copy(k):
        peer = to_node(k)
        return pltpu.make_async_remote_copy(
            src_ref=fetched.at[peer],
            dst_ref=table.at[node],
            send_sem=tab_send.at[peer],
            recv_sem=tab_recv.at[node],
            device_id=(peer, event),
            device_id_type=MESH,
        )

    for k in range(n_node - 1, 0, -1):
        table_copy(k).start()
    table[node] = fetched[node]

    pltpu.make_async_copy(feats, feats, feat_recv).wait()
    others = packs.at[pl.ds(0, shards - 1)]
    pltpu.make_async_copy(others, others, pack_recv).wait()
    for load in loads[1:]:
        load.wait()
    codes = packs[...].reshape(shards, LANES)
    code_parts = jnp.concatenate([codes >> 8, codes & 255], axis=1).astype(F32).astype(BF)
    kinds = 5
    from_lane = lax.broadcasted_iota(jnp.int32, (2 * LANES, kinds * LANES), 0)
    to_kind = lax.broadcasted_iota(jnp.int32, (2 * LANES, kinds * LANES), 1) // LANES
    weight = jnp.where(from_lane < LANES, 256.0, 1.0)
    gather_kind = jnp.where((from_lane % LANES) // slots == to_kind, weight, 0.0).astype(BF)

    @pl.loop(0, turns)
    def _(t):
        first = t * (chunk // slots)
        home = lax.broadcasted_iota(jnp.int32, (chunk, shards), 0) // slots + first
        from_home = one_hot(home == lax.broadcasted_iota(jnp.int32, (chunk, shards), 1))
        mine = mm(from_home, code_parts)
        lane = lax.broadcasted_iota(jnp.int32, (chunk, 2 * LANES), 1)
        slot = lax.broadcasted_iota(jnp.int32, (chunk, 2 * LANES), 0)
        mine = jnp.where(lane % slots == slot % slots, mine, 0.0).astype(BF)
        columns = mm(mine, gather_kind)
        times = columns[:, 3 * LANES : 4 * LANES]
        ids_col[t, 0] = columns[:, LANES : 2 * LANES].astype(jnp.int32)
        ids_col[t, 1] = columns[:, 2 * LANES : 3 * LANES].astype(jnp.int32)
        ids_col[t, 2] = columns[:, 4 * LANES :].astype(jnp.int32)
        for kind in range(3):
            line = columns[:, kind * LANES : (kind + 1) * LANES].T
            ids_row[t, kind] = line[:8].astype(jnp.int32)
        source = columns[:, :LANES].astype(jnp.int32)
        current = mm(pick_matrix(source, group_rows), mem[...]).astype(BF)
        from_state = mm(current, wst[...])
        timing = jnp.cos(times * freq_ref[...]).astype(BF)
        feature = feats[pl.ds(first, chunk // slots)].reshape(chunk, feat_ref.shape[2])
        from_rest = mm(jnp.concatenate([feature, timing], axis=1), win[width:, :])
        prev[t] = current
        recur[t] = from_state[:, 2 * width :]
        gates = from_rest[:, : 2 * width] + from_state[:, : 2 * width]
        pre[t] = jnp.concatenate([gates, from_rest[:, 2 * width :]], axis=1) + bias_ref[...]

    for k in range(1, n_node):
        arrived(table, tab_recv, to_node(k))
    table_grad[...] = jnp.zeros_like(table_grad)
    factor = 1.0 / math.sqrt(width)

    @pl.loop(0, turns)
    def _(t):
        rows_held = table[...].reshape(table_rows, width)
        partner = mm(pick_matrix(ids_col[t, 0], table_rows), rows_held).astype(BF)
        negative = mm(pick_matrix(ids_col[t, 1], table_rows), rows_held).astype(BF)
        valid = ids_col[t, 2].astype(F32)[:, :1]
        all_pre = pre[t] + mm(partner, win[:width, :])
        recurrent = recur[t]
        previous = prev[t].astype(F32)
        reset = jax.nn.sigmoid(all_pre[:, :width])
        update = jax.nn.sigmoid(all_pre[:, width : 2 * width])
        candidate = jnp.tanh(all_pre[:, 2 * width :] + reset * recurrent)
        renewed = (1.0 - update) * candidate + update * previous
        key_pos = mm(partner, wpair[...])
        key_neg = mm(negative, wpair[...])
        score_pos = jnp.sum(renewed * key_pos, axis=1, keepdims=True) * factor
        score_neg = jnp.sum(renewed * key_neg, axis=1, keepdims=True) * factor
        weight_pos = -valid * jax.nn.sigmoid(-score_pos)
        weight_neg = valid * jax.nn.sigmoid(score_neg)
        grad_renewed = (weight_pos * key_pos + weight_neg * key_neg) * factor
        grad_keypos = (weight_pos * renewed * factor).astype(BF)
        grad_keyneg = (weight_neg * renewed * factor).astype(BF)
        grad_cand = grad_renewed * (1.0 - update) * (1.0 - candidate * candidate)
        grad_reset = (grad_cand * recurrent * reset * (1.0 - reset)).astype(BF)
        grad_update = (
            grad_renewed * (previous - candidate) * update * (1.0 - update)
        ).astype(BF)
        input_back = jnp.concatenate([grad_reset, grad_update, grad_cand.astype(BF)], axis=1)
        state_back = jnp.concatenate(
            [grad_reset, grad_update, (grad_cand * reset).astype(BF)], axis=1
        )
        grad_partner = mm_nt(input_back, win[:width, :]) + mm_nt(grad_keypos, wpair[...])
        grad_negative = mm_nt(grad_keyneg, wpair[...])
        high, low = split(jnp.concatenate([grad_partner, grad_negative], axis=0))
        spread = jnp.concatenate(
            [
                spread_matrix(ids_row[t, 1][:1], table_rows, 0),
                spread_matrix(ids_row[t, 2][:1], table_rows, 0),
            ],
            axis=1,
        )
        table_grad[...] += mm(spread, high) + mm(spread, low)
        grad_current = grad_renewed * update + mm_nt(state_back, wst[...])
        high, low = split(grad_current)
        cur_high[t] = high
        cur_low[t] = low

    high, low = split(table_grad[...])
    back_out[...] = high.reshape(n_node, asked, width)

    def back_copy(k):
        peer = to_node(k)
        return pltpu.make_async_remote_copy(
            src_ref=back_out.at[peer],
            dst_ref=back_in.at[node],
            send_sem=back_send.at[peer],
            recv_sem=back_recv.at[node],
            device_id=(peer, event),
            device_id_type=MESH,
        )

    for k in range(n_node - 1, 0, -1):
        back_copy(k).start()
    table_grad[...] = low.astype(F32)
    own_low[...] = table_grad[pl.ds(pl.multiple_of(node * asked, asked), asked), :].astype(BF)
    back_in[node] = back_out[node]

    @pl.loop(0, n_event)
    def _(b):
        total = mm(spread_matrix(wanted[node], block, b * block), own_low[...])
        for t in range(turns):
            spread = spread_matrix(ids_row[t, 0][:1], block, b * block)
            total += mm(spread, cur_high[t]) + mm(spread, cur_low[t])
        acc[b] = total

    for k in range(1, n_node):
        arrived(back_in, back_recv, to_node(k))
    returned = back_in[...].reshape(table_rows, width)
    listed = jnp.concatenate([wanted[g] for g in range(n_node)], axis=1)

    def whole_block(b):
        return acc[b] + mm(spread_matrix(listed, block, b * block), returned)

    def pair_copy(j):
        return pltpu.make_async_remote_copy(
            src_ref=pair_out.at[j],
            dst_ref=pair_in.at[j],
            send_sem=pair_send.at[j],
            recv_sem=pair_recv.at[j],
            device_id=(node, sibling),
            device_id_type=MESH,
        )

    def block_copy(j):
        return pltpu.make_async_remote_copy(
            src_ref=block_out.at[j],
            dst_ref=block_in.at[chip],
            send_sem=block_send.at[j],
            recv_sem=block_recv.at[chip],
            device_id=(node, 2 * j + core),
            device_id_type=MESH,
        )

    @pl.loop(1, chips + 1)
    def _(k):
        j = lax.rem(chip + k, chips)
        pair_out[j] = whole_block(2 * j + 1 - core)
        pair_copy(j).start()

    @pl.loop(1, chips)
    def _(k):
        j = lax.rem(chip + k, chips)
        total = whole_block(2 * j + core)
        arrived(pair_in, pair_recv, j)
        block_out[j] = (total + pair_in[j]).astype(BF)
        block_copy(j).start()

    total = whole_block(event)
    arrived(pair_in, pair_recv, chip)
    total += pair_in[chip]
    for k in range(1, chips):
        j = lax.rem(chip + k, chips)
        arrived(block_in, block_recv, j)
        total += block_in[j].astype(F32)
    out_ref[...] = total

    for k in range(1, n_node):
        request_copy(k).wait_send()
        table_copy(k).wait_send()
        back_copy(k).wait_send()
    for k in range(1, chips):
        block_copy(lax.rem(chip + k, chips)).wait_send()
    for j in range(chips):
        pair_copy(j).wait_send()
    sent = feats.at[pl.ds(0, shards - 1)]
    pltpu.make_async_copy(sent, sent, feat_send).wait()
    pltpu.make_async_copy(others, others, pack_send).wait()


def local(
    memory,
    event_feat,
    event_source,
    event_partner,
    event_negative,
    event_time,
    event_count,
    requests,
    w_input,
    w_state,
    w_pair,
    gate_bias,
    time_freq,
):
    n_node = lax.axis_size("node")
    n_event = lax.axis_size("event")
    shards = n_node * n_event
    slots, feat_width = event_feat.shape[2:]
    group_rows, width = memory.shape
    asked = requests.shape[2]
    table_rows = n_node * asked
    events = shards * slots
    chunk = math.gcd(events, 512)
    turns = events // chunk
    chips = n_event // 2
    block = group_rows // n_event

    live = (jnp.arange(slots, dtype=jnp.int32)[None, :] < event_count[0][:, None]).astype(jnp.int32)
    parts = [event_source[0], event_partner[0], event_negative[0], event_time[0], live]
    parts.append(jnp.zeros((shards, LANES - 5 * slots), jnp.int32))
    packed = jnp.concatenate(parts, axis=1).reshape(shards, 1, LANES)

    vmem = pl.BlockSpec(memory_space=pltpu.VMEM)
    hbm = pl.BlockSpec(memory_space=pl.ANY)
    dma = pltpu.SemaphoreType.DMA
    return pl.pallas_call(
        functools.partial(kernel, n_node, n_event, chunk),
        out_shape=jax.ShapeDtypeStruct((block, width), F32),
        in_specs=[vmem, hbm, vmem, hbm, hbm, hbm, hbm, vmem, vmem],
        out_specs=vmem,
        scratch_shapes=[
            pltpu.VMEM(memory.shape, BF),
            pltpu.VMEM(w_input.shape, BF),
            pltpu.VMEM(w_state.shape, BF),
            pltpu.VMEM(w_pair.shape, BF),
            pltpu.VMEM((shards, slots, feat_width), BF),
            pltpu.VMEM((shards, 1, LANES), jnp.int32),
            pltpu.VMEM((n_node, 1, asked), jnp.int32),
            pltpu.VMEM((n_node, asked, width), BF),
            pltpu.VMEM((n_node, asked, width), BF),
            pltpu.VMEM((turns, chunk, 3 * width), F32),
            pltpu.VMEM((turns, chunk, width), F32),
            pltpu.VMEM((turns, chunk, width), BF),
            pltpu.VMEM((turns, 3, 8, chunk), jnp.int32),
            pltpu.VMEM((turns, 3, chunk, LANES), jnp.int32),
            pltpu.VMEM((table_rows, width), F32),
            pltpu.VMEM((turns, chunk, width), BF),
            pltpu.VMEM((turns, chunk, width), BF),
            pltpu.VMEM((n_node, asked, width), BF),
            pltpu.VMEM((n_node, asked, width), BF),
            pltpu.VMEM((asked, width), BF),
            pltpu.VMEM((n_event, block, width), F32),
            pltpu.VMEM((chips, block, width), F32),
            pltpu.VMEM((chips, block, width), F32),
            pltpu.VMEM((chips, block, width), BF),
            pltpu.VMEM((chips, block, width), BF),
            dma((4,)),
            dma,
            dma,
            dma,
            dma,
            dma((n_node,)),
            dma((n_node,)),
            dma((n_node,)),
            dma((n_node,)),
            dma((n_node,)),
            dma((n_node,)),
            dma((chips,)),
            dma((chips,)),
            dma((chips,)),
            dma((chips,)),
        ],
        compiler_params=pltpu.CompilerParams(
            collective_id=0, has_side_effects=True, vmem_limit_bytes=56 * 1024 * 1024
        ),
        name="memory_step",
    )(
        packed,
        event_feat[0],
        requests[0][:, None, :],
        memory,
        w_input,
        w_state,
        w_pair,
        gate_bias[None, :],
        time_freq[None, :],
    )


def solution(mesh):
    by_device = ("node", "event")
    in_specs = (
        P("node", None),
        P(by_device, None, None, None),
        P(by_device, None, None),
        P(by_device, None, None),
        P(by_device, None, None),
        P(by_device, None, None),
        P(by_device, None),
        P(by_device, None, None),
        P(),
        P(),
        P(),
        P(),
        P(),
    )
    out_specs = P(by_device, None)
    return jax.shard_map(local, mesh=mesh, in_specs=in_specs, out_specs=out_specs, check_vma=False)
```

time: 185 us -> 46.6 us (0.25)
  waiting for transfers between devices: 85.5 us -> 0 us
  Pallas kernels: 0 us -> 39.7 us
  matrix products: 27.6 us -> 0 us
  starting transfers between devices: 26.1 us -> 0 us
  blocking collectives: 14.2 us -> 0 us
  between operations: 13.7 us -> 0.02 us
  other arithmetic: 6.27 us -> 0.07 us
  local copies, waits for them, and re-layouts: 11.1 us -> 6.46 us
    all_to_all x8 -> x0, waiting for transfers between devices: 46.9 us -> none  [the longest x1 11.3 us: local(): lax.all_to_all(table_grad.reshape(incoming.shape + (width,)), 'node', spl...]
    pallas_call x0 -> x1, Pallas kernels: none -> 39.7 us  [local(): pl.pallas_call(functools.partial(kernel, n_node, n_event, chunk), out_sha...]
    reduce_scatter x1 -> x0, waiting for transfers between devices: 38.6 us -> none  [local(): lax.psum_scatter(state_grad, 'event', scatter_dimension=0, tiled=True)]
    dot_general x15 -> x0, matrix products: 27.6 us -> none  [the longest x4 11.6 us: add_rows(): lax.dot_general(selector, grads, (((0,), (0,)), ((), ())), precision=lax....]
    all_to_all x8 -> x0, starting transfers between devices: 25.8 us -> none  [the longest x1 4.93 us: local(): lax.all_to_all(event_time, ('node', 'event'), split_axis=1, concat_axis=0...]
    all_to_all x1 -> x0, blocking collectives: 14.2 us -> none  [local(): lax.all_to_all(event_count, ('node', 'event'), split_axis=1, concat_axis=...]
    all_to_all x4 -> x0, other arithmetic: 2.46 us -> none  [the longest x1 0.66 us: local(): lax.all_to_all(event_count, ('node', 'event'), split_axis=1, concat_axis=...]
    unnamed x42 -> x17, local copies, waits for them, and re-layouts: 6.59 us -> 5.18 us
  transfers between devices with their start and end apart: 9 -> 0, of which waited for: 9 -> 0; matrix products, arithmetic and copies ran while one was open for 10% -> 0% of each run, Pallas kernels for 0% -> 0%
where the time goes in v1:
time: 46.6 us; the launch traced here: 46.2 us
  Pallas kernels  39.7 us (85%)
  local copies, waits for them, and re-layouts  6.46 us (14%)
    pallas_call x1, Pallas kernels, local(): pl.pallas_call(functools.partial(kernel, n_node, n_event, chunk), out_sha...  39.7 us
    unnamed x17, local copies, waits for them, and re-layouts  5.18 us

profile of v1, /device:TPU:0, one launch (start us, length us, event | category | flops | bytes accessed | tf_op | source)
XLA Modules:
  0.0 46.2 jit_solution(15001817266098217436)
XLA Ops:
  0.0 0.0 copy-start.4
  0.0 0.0 copy-start
  0.0 0.7 %copy-done.4 = f32[768]{0:T(1024)S(1)} copy-done((f32[768]{0:T(1024)S(1)}, f32[768]{0:T(1024)}, u32[]{:S(2)}) %copy-start.4) | copy-done | bytes 3096
  0.7 0.6 %broadcast_in_dim.11.bias_ref = f32[1,768]{1,0:T(1,128)} reshape(f32[768]{0:T(1024)S(1)} %copy-done.4) | data formatting | bytes 6144 | tf_op jit(solution)/shard_map/broadcast_in_dim | solution.py:485
  1.3 0.0 copy-done
  1.3 0.0 copy-start.1
  1.3 0.1 copy.14
  1.4 0.6 %copy-done.1 = s32[1,32,16]{1,2,0:T(8,128)S(1)} copy-done((s32[1,32,16]{1,2,0:T(8,128)S(1)}, s32[1,32,16]{1,2,0:T(8,128)}, u32[]{:S(2)}) %copy-start.1) | copy-done | bytes 2072
  2.0 0.0 copy-start.2
  2.0 0.1 copy.15
  2.1 0.6 %copy-done.2 = s32[1,32,16]{1,2,0:T(8,128)S(1)} copy-done((s32[1,32,16]{1,2,0:T(8,128)S(1)}, s32[1,32,16]{1,2,0:T(8,128)}, u32[]{:S(2)}) %copy-start.2) | copy-done | bytes 2072
  2.7 0.0 copy-start.3
  2.7 0.1 copy.16
  2.8 0.6 %copy-done.3 = s32[1,32,16]{1,2,0:T(8,128)S(1)} copy-done((s32[1,32,16]{1,2,0:T(8,128)S(1)}, s32[1,32,16]{1,2,0:T(8,128)}, u32[]{:S(2)}) %copy-start.3) | copy-done | bytes 2072
  3.4 0.1 copy.17
  3.4 0.0 copy-start.5
  3.4 0.7 %copy-done.5 = s32[1,32]{1,0:T(1,128)S(1)} copy-done((s32[1,32]{1,0:T(1,128)S(1)}, s32[1,32]{1,0:T(1,128)}, u32[]{:S(2)}) %copy-start.5) | copy-done | bytes 152
  4.1 0.1 fusion
  4.2 0.7 %concatenate.3 = s32[32,128]{1,0:T(8,128)} concatenate(s32[32,16]{1,0:T(8,128)S(1)} %bitcast.11, s32[32,16]{1,0:T(8,128)S(1)} %bitcast.12, s32[32,16]{1,0:T(8,128)S(1)} %bitcast.13, s32[32,16]{1,0:T(8,128)S(1)} %bitcast.14, s32[32,16]{1,0:T(8,128)S(1)} %fusion, s32[32,48]{1,0:T(8,128)S(1)} %broadcast_in_dim.10), dimensions={1} | concatenate | bytes 32768 | tf_op jit(solution)/shard_map/concatenate | solution.py:421
  4.9 39.7 %memory_step.1 = f32[256,256]{1,0:T(8,128)} custom-call(s32[32,1,128]{2,1,0:T(1,128)} %bitcast.10, bf16[32,16,128]{2,1,0:T(8,128)(2,1)} %bitcast.9, s32[4,1,128]{2,1,0:T(1,128)} %bitcast.15, bf16[2048,256]{1,0:T(8,128)(2,1)} %mem_hbm.1, bf16[512,768]{1,0:T(8,128)(2,1)} %win_hbm.1, bf16[256,768]{1,0:T(8,128)(2,1)} %wst_hbm.1, bf16[256,256]{1,0:T(8,128)(2,1)} %wpair_hbm.1, ...), custom_call_target="tpu_custom_call" | custom-call | tf_op jit(solution)/shard_map/memory_step/pallas_call | solution.py:426
  44.6 1.7 %copy.19 = f32[256,256]{1,0:T(8,128)} copy(f32[256,256]{1,0:T(8,128)} %memory_step.1) | data formatting | bytes 524288
  (1 shorter events, 0.0 us)
Async XLA Ops:
  0.0 0.7 %copy-start.4 = (f32[768]{0:T(1024)S(1)}, f32[768]{0:T(1024)}, u32[]{:S(2)}) copy-start(f32[768]{0:T(1024)} %param.24) | copy-start | bytes 9220
  0.0 1.3 %copy-start = (s32[1,32,16]{1,2,0:T(8,128)S(1)}, s32[1,32,16]{1,2,0:T(8,128)}, u32[]{:S(2)}) copy-start(s32[1,32,16]{1,2,0:T(8,128)} %param.15) | copy-start | bytes 6148
  1.3 0.7 %copy-start.1 = (s32[1,32,16]{1,2,0:T(8,128)S(1)}, s32[1,32,16]{1,2,0:T(8,128)}, u32[]{:S(2)}) copy-start(s32[1,32,16]{1,2,0:T(8,128)} %param.16) | copy-start | bytes 6148
  2.0 0.7 %copy-start.2 = (s32[1,32,16]{1,2,0:T(8,128)S(1)}, s32[1,32,16]{1,2,0:T(8,128)}, u32[]{:S(2)}) copy-start(s32[1,32,16]{1,2,0:T(8,128)} %param.17) | copy-start | bytes 6148
  2.7 0.7 %copy-start.3 = (s32[1,32,16]{1,2,0:T(8,128)S(1)}, s32[1,32,16]{1,2,0:T(8,128)}, u32[]{:S(2)}) copy-start(s32[1,32,16]{1,2,0:T(8,128)} %param.18) | copy-start | bytes 6148
  3.4 0.7 %copy-start.5 = (s32[1,32]{1,0:T(1,128)S(1)}, s32[1,32]{1,0:T(1,128)}, u32[]{:S(2)}) copy-start(s32[1,32]{1,0:T(1,128)} %param.19) | copy-start | bytes 388

commit v2 on v1

v2 whole, which is shorter than its diff:
```python
import functools
import math

import jax
import jax.numpy as jnp
from jax import lax
from jax.experimental import pallas as pl
from jax.experimental.pallas import tpu as pltpu
from jax.sharding import PartitionSpec as P

MESH = pl.DeviceIdType.MESH
BF = jnp.bfloat16
F32 = jnp.float32
LANES = 128
OUT = pltpu.VMEM


def mm(a, b):
    return jnp.dot(a, b, preferred_element_type=F32)


def mm_nt(a, b):
    return lax.dot_general(a, b, (((1,), (1,)), ((), ())), preferred_element_type=F32)


def split(value):
    high = value.astype(BF)
    return high, (value - high.astype(F32)).astype(BF)


def one_hot(mask):
    return jnp.where(mask, 1.0, 0.0).astype(BF)


def pick_matrix(column, total):
    lane = lax.broadcasted_iota(jnp.int32, column.shape, 1)
    return jnp.concatenate(
        [one_hot(column == lane + start) for start in range(0, total, LANES)], axis=1
    )


def spread_matrix(row, total, base):
    ids = lax.broadcasted_iota(jnp.int32, (total, row.shape[1]), 0) + base
    return one_hot(ids == row)


def kernel(
    n_node,
    n_event,
    chunk,
    ids_hbm,
    count_hbm,
    feat_ref,
    req_ref,
    mem_hbm,
    win_hbm,
    wst_hbm,
    wpair_hbm,
    bias_hbm,
    freq_hbm,
    out_ref,
    mem,
    win,
    wst,
    wpair,
    bias,
    freq,
    ids,
    count,
    stage,
    pack,
    feats,
    packs,
    wanted,
    wanted_pair,
    fetched,
    table,
    pre,
    recur,
    prev,
    ids_row,
    source_row,
    source_pair,
    live,
    pick,
    spread,
    place,
    table_grad,
    renew_grad,
    state_grad,
    cur,
    cur_pair,
    back_out,
    back_in,
    back_pair,
    acc,
    block_out,
    block_in,
    load_sem,
    feat_send,
    feat_recv,
    pack_send,
    pack_recv,
    req_send,
    req_recv,
    tab_send,
    tab_recv,
    list_send,
    list_recv,
    cur_send,
    cur_recv,
    back_send,
    back_recv,
    pass_send,
    pass_recv,
    block_send,
    block_recv,
):
    shards = n_node * n_event
    node, event = lax.axis_index("node"), lax.axis_index("event")
    me = node * n_event + event
    slots = feat_ref.shape[1]
    width = mem.shape[1]
    group_rows = mem.shape[0]
    asked = req_ref.shape[2]
    table_rows = n_node * asked
    events = shards * slots
    turns = events // chunk
    chips = n_event // 2
    chip, core = event // 2, event % 2
    sibling = event + 1 - 2 * core
    block = group_rows // n_event
    half = width // 2

    barrier = pltpu.get_barrier_semaphore()

    @pl.loop(1, shards)
    def _(k):
        peer = lax.rem(me + k, shards)
        pl.semaphore_signal(
            barrier, inc=1, device_id=(peer // n_event, peer % n_event), device_id_type=MESH
        )

    small = [
        pltpu.make_async_copy(ids_hbm[k], ids.at[k], load_sem.at[k]) for k in range(4)
    ] + [pltpu.make_async_copy(count_hbm, count, load_sem.at[4])]
    loads = [
        pltpu.make_async_copy(source, target, load_sem.at[5 + k])
        for k, (source, target) in enumerate(
            (
                (mem_hbm, mem),
                (win_hbm, win),
                (wst_hbm, wst),
                (wpair_hbm, wpair),
                (bias_hbm, bias),
                (freq_hbm, freq),
            )
        )
    ]
    own_list = pltpu.make_async_copy(req_ref.at[node], wanted.at[node], req_recv.at[node])
    own_feat = pltpu.make_async_copy(feat_ref.at[me], feats.at[me], feat_recv)
    for load in small + loads + [own_list, own_feat]:
        load.start()
    stage[...] = jnp.zeros_like(stage)
    for load in small:
        load.wait()
    for k in range(4):
        stage[k * slots : (k + 1) * slots, :shards] = ids[k]
    slot = lax.broadcasted_iota(jnp.int32, (slots, shards), 0)
    stage[4 * slots : 5 * slots, :shards] = jnp.where(slot < count[...], 1, 0)
    pack[...] = stage[...].T[:shards].reshape(shards, 1, LANES)
    packs[me] = pack[me]
    pl.semaphore_wait(barrier, shards - 1)

    def to_node(k):
        return lax.rem(node + k, n_node)

    def arrived(buffer, sem, slot):
        pltpu.make_async_copy(buffer.at[slot], buffer.at[slot], sem.at[slot]).wait()

    def request_copy(k):
        peer = to_node(k)
        return pltpu.make_async_remote_copy(
            src_ref=req_ref.at[peer],
            dst_ref=wanted.at[node],
            send_sem=req_send.at[peer],
            recv_sem=req_recv.at[node],
            device_id=(peer, event),
            device_id_type=MESH,
        )

    for k in range(n_node - 1, 0, -1):
        request_copy(k).start()

    @pl.loop(1, shards)
    def _(k):
        peer = lax.rem(me + k, shards)
        target = (peer // n_event, peer % n_event)
        pltpu.make_async_remote_copy(
            src_ref=pack.at[peer],
            dst_ref=packs.at[me],
            send_sem=pack_send,
            recv_sem=pack_recv,
            device_id=target,
            device_id_type=MESH,
        ).start()
        pltpu.make_async_remote_copy(
            src_ref=feat_ref.at[peer],
            dst_ref=feats.at[me],
            send_sem=feat_send,
            recv_sem=feat_recv,
            device_id=target,
            device_id_type=MESH,
        ).start()

    for k in range(n_node):
        arrived(wanted, req_recv, to_node(k))
    loads[0].wait()
    columns = [jnp.broadcast_to(wanted[g], (LANES, asked)).T for g in range(n_node)]
    picked = mm(pick_matrix(jnp.concatenate(columns, axis=0), group_rows), mem[...]).astype(BF)
    fetched[...] = picked.reshape(n_node, asked, width)

    def table_copy(k):
        peer = to_node(k)
        return pltpu.make_async_remote_copy(
            src_ref=fetched.at[peer],
            dst_ref=table.at[node],
            send_sem=tab_send.at[peer],
            recv_sem=tab_recv.at[node],
            device_id=(peer, event),
            device_id_type=MESH,
        )

    for k in range(n_node - 1, 0, -1):
        table_copy(k).start()
    table[node] = fetched[node]

    def to_sibling(source, target, send_sem, recv_sem):
        return pltpu.make_async_remote_copy(
            src_ref=source,
            dst_ref=target,
            send_sem=send_sem,
            recv_sem=recv_sem,
            device_id=(node, sibling),
            device_id_type=MESH,
        )

    wanted_copy = to_sibling(wanted, wanted_pair, list_send.at[0], list_recv.at[0])
    wanted_copy.start()

    pltpu.make_async_copy(feats, feats, feat_recv).wait()
    others = packs.at[pl.ds(0, shards - 1)]
    pltpu.make_async_copy(others, others, pack_recv).wait()
    for load in loads[1:]:
        load.wait()
    codes = packs[...].reshape(shards, LANES)
    code_parts = jnp.concatenate([codes >> 8, codes & 255], axis=1).astype(F32).astype(BF)
    kinds = 5
    from_lane = lax.broadcasted_iota(jnp.int32, (2 * LANES, kinds * LANES), 0)
    to_kind = lax.broadcasted_iota(jnp.int32, (2 * LANES, kinds * LANES), 1) // LANES
    weight = jnp.where(from_lane < LANES, 256.0, 1.0)
    gather_kind = jnp.where((from_lane % LANES) // slots == to_kind, weight, 0.0).astype(BF)
    bias_row = jnp.concatenate([bias[k : k + 1, :] for k in range(bias.shape[0])], axis=1)

    @pl.loop(0, turns)
    def _(t):
        first = t * (chunk // slots)
        home = lax.broadcasted_iota(jnp.int32, (chunk, shards), 0) // slots + first
        from_home = one_hot(home == lax.broadcasted_iota(jnp.int32, (chunk, shards), 1))
        mine = mm(from_home, code_parts)
        lane = lax.broadcasted_iota(jnp.int32, (chunk, 2 * LANES), 1)
        row = lax.broadcasted_iota(jnp.int32, (chunk, 2 * LANES), 0)
        mine = jnp.where(lane % slots == row % slots, mine, 0.0).astype(BF)
        columns = mm(mine, gather_kind)
        times = columns[:, 3 * LANES : 4 * LANES]
        live[t] = columns[:, 4 * LANES :]
        for kind in range(2):
            line = columns[:, (kind + 1) * LANES : (kind + 2) * LANES].T
            ids_row[t, kind] = line[:8].astype(jnp.int32)
        source_row[t] = columns[:, :LANES].T[:8].astype(jnp.int32)
        source = columns[:, :LANES].astype(jnp.int32)
        current = mm(pick_matrix(source, group_rows), mem[...]).astype(BF)
        from_state = mm(current, wst[...])
        timing = jnp.cos(times * freq[...]).astype(BF)
        feature = feats[pl.ds(first, chunk // slots)].reshape(chunk, feat_ref.shape[2])
        from_rest = mm(jnp.concatenate([feature, timing], axis=1), win[width:, :])
        prev[t] = current
        recur[t] = from_state[:, 2 * width :]
        gates = from_rest[:, : 2 * width] + from_state[:, : 2 * width]
        pre[t] = jnp.concatenate([gates, from_rest[:, 2 * width :]], axis=1) + bias_row
        for kind in range(2):
            column = columns[:, (kind + 1) * LANES : (kind + 2) * LANES].astype(jnp.int32)
            pick[t, kind * chunk : (kind + 1) * chunk] = pick_matrix(column, table_rows)
            spread[t, :, kind * chunk : (kind + 1) * chunk] = spread_matrix(
                ids_row[t, kind][:1], table_rows, 0
            )

    source_copy = to_sibling(source_row, source_pair, list_send.at[1], list_recv.at[1])
    source_copy.start()
    arrived_pair = pltpu.make_async_copy(wanted_pair, wanted_pair, list_recv.at[0])
    arrived_pair.wait()
    listed = jnp.concatenate(
        [wanted[g] for g in range(n_node)]
        + [wanted[node]]
        + [wanted_pair[g] for g in range(n_node)]
        + [wanted_pair[node]],
        axis=1,
    )

    @pl.loop(0, chips)
    def _(j):
        place[j] = spread_matrix(listed, block, (2 * j + core) * block)

    for k in range(1, n_node):
        arrived(table, tab_recv, to_node(k))
    table_grad[...] = jnp.zeros_like(table_grad)
    factor = 1.0 / math.sqrt(width)

    @pl.loop(0, turns)
    def _(t):
        rows = mm(pick[t], table[...].reshape(table_rows, width)).astype(BF)
        partner = rows[:chunk]
        valid = live[t][:, :1]
        all_pre = pre[t] + mm(partner, win[:width, :])
        recurrent = recur[t]
        previous = prev[t].astype(F32)
        reset = jax.nn.sigmoid(all_pre[:, :width])
        update = jax.nn.sigmoid(all_pre[:, width : 2 * width])
        candidate = jnp.tanh(all_pre[:, 2 * width :] + reset * recurrent)
        renewed = (1.0 - update) * candidate + update * previous
        keys = mm(rows, wpair[...])
        key_pos, key_neg = keys[:chunk], keys[chunk:]
        score_pos = jnp.sum(renewed * key_pos, axis=1, keepdims=True) * factor
        score_neg = jnp.sum(renewed * key_neg, axis=1, keepdims=True) * factor
        weight_pos = -valid * jax.nn.sigmoid(-score_pos)
        weight_neg = valid * jax.nn.sigmoid(score_neg)
        grad_renewed = (weight_pos * key_pos + weight_neg * key_neg) * factor
        grad_keypos = (weight_pos * renewed * factor).astype(BF)
        grad_keyneg = (weight_neg * renewed * factor).astype(BF)
        grad_cand = grad_renewed * (1.0 - update) * (1.0 - candidate * candidate)
        grad_reset = (grad_cand * recurrent * reset * (1.0 - reset)).astype(BF)
        grad_update = (
            grad_renewed * (previous - candidate) * update * (1.0 - update)
        ).astype(BF)
        input_back = jnp.concatenate([grad_reset, grad_update, grad_cand.astype(BF)], axis=1)
        renew_grad[t] = grad_renewed * update
        state_grad[t] = jnp.concatenate(
            [grad_reset, grad_update, (grad_cand * reset).astype(BF)], axis=1
        )
        grad_keys = mm_nt(jnp.concatenate([grad_keypos, grad_keyneg], axis=0), wpair[...])
        grad_partner = mm_nt(input_back, win[:width, :]) + grad_keys[:chunk]
        high, low = split(jnp.concatenate([grad_partner, grad_keys[chunk:]], axis=0))
        table_grad[...] += mm(spread[t], high) + mm(spread[t], low)

    high, low = split(table_grad[...])
    for h in range(2):
        back_out[h] = high[:, h * half : (h + 1) * half].reshape(n_node, asked, half)

    def back_copy(h, k):
        peer = to_node(k)
        return pltpu.make_async_remote_copy(
            src_ref=back_out.at[h, peer],
            dst_ref=back_in.at[h, node],
            send_sem=back_send.at[h, peer],
            recv_sem=back_recv.at[h, node],
            device_id=(peer, event),
            device_id_type=MESH,
        )

    def pass_copy(h, slot):
        return to_sibling(
            back_in.at[h, slot],
            back_pair.at[h, slot],
            pass_send.at[h, slot],
            pass_recv.at[h, slot],
        )

    for h in range(2):
        for k in range(n_node - 1, 0, -1):
            back_copy(h, k).start()
    table_grad[...] = low.astype(F32)
    own_low = table_grad[pl.ds(pl.multiple_of(node * asked, asked), asked), :].astype(BF)
    for h in range(2):
        back_in[h, node] = back_out[h, node]
        back_in[h, n_node] = own_low[:, h * half : (h + 1) * half]
        pass_copy(h, node).start()
        pass_copy(h, n_node).start()

    @pl.loop(0, turns)
    def _(t):
        high, low = split(renew_grad[t] + mm_nt(state_grad[t], wst[...]))
        cur[t, 0] = high
        cur[t, 1] = low

    cur_copy = to_sibling(cur, cur_pair, cur_send, cur_recv)
    cur_copy.start()

    @pl.loop(0, chips)
    def _(j):
        total = jnp.zeros((block, width), F32)
        for t in range(turns):
            at = spread_matrix(source_row[t][:1], block, (2 * j + core) * block)
            total += mm(at, cur[t, 0]) + mm(at, cur[t, 1])
        acc[j] = total

    pltpu.make_async_copy(source_pair, source_pair, list_recv.at[1]).wait()
    pltpu.make_async_copy(cur_pair, cur_pair, cur_recv).wait()

    @pl.loop(0, chips)
    def _(j):
        total = acc[j]
        for t in range(turns):
            at = spread_matrix(source_pair[t][:1], block, (2 * j + core) * block)
            total += mm(at, cur_pair[t, 0]) + mm(at, cur_pair[t, 1])
        acc[j] = total

    def block_copy(h, j):
        return pltpu.make_async_remote_copy(
            src_ref=block_out.at[h, j],
            dst_ref=block_in.at[h, chip],
            send_sem=block_send.at[h, j],
            recv_sem=block_recv.at[h, chip],
            device_id=(node, 2 * j + core),
            device_id_type=MESH,
        )

    own = []
    for h in range(2):
        for k in range(1, n_node):
            slot = to_node(k)
            arrived(back_in.at[h], back_recv.at[h], slot)
            pass_copy(h, slot).start()
        for slot in range(n_node + 1):
            arrived(back_pair.at[h], pass_recv.at[h], slot)
        rows = (n_node + 1) * asked
        returned = jnp.concatenate(
            [back_in[h].reshape(rows, half), back_pair[h].reshape(rows, half)], axis=0
        )

        def whole_block(j):
            return acc[j][:, h * half : (h + 1) * half] + mm(place[j], returned)

        @pl.loop(1, chips)
        def _(k):
            j = lax.rem(chip + k, chips)
            block_out[h, j] = whole_block(j).astype(BF)
            block_copy(h, j).start()

        own.append(whole_block(chip))

    for h in range(2):
        total = own[h]
        for k in range(1, chips):
            j = lax.rem(chip + k, chips)
            arrived(block_in.at[h], block_recv.at[h], j)
            total += block_in[h, j].astype(F32)
        out_ref[:, h * half : (h + 1) * half] = total

    for k in range(1, n_node):
        request_copy(k).wait_send()
        table_copy(k).wait_send()
    for h in range(2):
        for k in range(1, n_node):
            back_copy(h, k).wait_send()
        for slot in range(n_node + 1):
            pass_copy(h, slot).wait_send()
        for k in range(1, chips):
            block_copy(h, lax.rem(chip + k, chips)).wait_send()
    wanted_copy.wait_send()
    source_copy.wait_send()
    cur_copy.wait_send()
    sent = feats.at[pl.ds(0, shards - 1)]
    pltpu.make_async_copy(sent, sent, feat_send).wait()
    pltpu.make_async_copy(others, others, pack_send).wait()


def local(
    memory,
    event_feat,
    event_source,
    event_partner,
    event_negative,
    event_time,
    event_count,
    requests,
    w_input,
    w_state,
    w_pair,
    gate_bias,
    time_freq,
):
    n_node = lax.axis_size("node")
    n_event = lax.axis_size("event")
    shards = n_node * n_event
    slots, feat_width = event_feat.shape[2:]
    group_rows, width = memory.shape
    asked = requests.shape[2]
    table_rows = n_node * asked
    events = shards * slots
    chunk = math.gcd(events, 512)
    turns = events // chunk
    chips = n_event // 2
    block = group_rows // n_event
    half = width // 2
    listed = (n_node + 1) * asked
    bias_rows = gate_bias.shape[0] // LANES

    vmem = pl.BlockSpec(memory_space=pltpu.VMEM)
    hbm = pl.BlockSpec(memory_space=pl.ANY)
    dma = pltpu.SemaphoreType.DMA
    ids = [value[0].T for value in (event_source, event_partner, event_negative, event_time)]
    return pl.pallas_call(
        functools.partial(kernel, n_node, n_event, chunk),
        out_shape=OUT((block, width), F32),
        in_specs=[[hbm] * 4] + [hbm] * 9,
        out_specs=vmem,
        scratch_shapes=[
            pltpu.VMEM(memory.shape, BF),
            pltpu.VMEM(w_input.shape, BF),
            pltpu.VMEM(w_state.shape, BF),
            pltpu.VMEM(w_pair.shape, BF),
            pltpu.VMEM((bias_rows, LANES), F32),
            pltpu.VMEM((1, LANES), F32),
            pltpu.VMEM((4, slots, shards), jnp.int32),
            pltpu.VMEM((1, shards), jnp.int32),
            pltpu.VMEM((LANES, max(shards, LANES)), jnp.int32),
            pltpu.VMEM((shards, 1, LANES), jnp.int32),
            pltpu.VMEM((shards, slots, feat_width), BF),
            pltpu.VMEM((shards, 1, LANES), jnp.int32),
            pltpu.VMEM((n_node, 1, asked), jnp.int32),
            pltpu.VMEM((n_node, 1, asked), jnp.int32),
            pltpu.VMEM((n_node, asked, width), BF),
            pltpu.VMEM((n_node, asked, width), BF),
            pltpu.VMEM((turns, chunk, 3 * width), F32),
            pltpu.VMEM((turns, chunk, width), F32),
            pltpu.VMEM((turns, chunk, width), BF),
            pltpu.VMEM((turns, 2, 8, chunk), jnp.int32),
            pltpu.VMEM((turns, 8, chunk), jnp.int32),
            pltpu.VMEM((turns, 8, chunk), jnp.int32),
            pltpu.VMEM((turns, chunk, LANES), F32),
            pltpu.VMEM((turns, 2 * chunk, table_rows), BF),
            pltpu.VMEM((turns, table_rows, 2 * chunk), BF),
            pltpu.VMEM((chips, block, 2 * listed), BF),
            pltpu.VMEM((table_rows, width), F32),
            pltpu.VMEM((turns, chunk, width), F32),
            pltpu.VMEM((turns, chunk, 3 * width), BF),
            pltpu.VMEM((turns, 2, chunk, width), BF),
            pltpu.VMEM((turns, 2, chunk, width), BF),
            pltpu.VMEM((2, n_node, asked, half), BF),
            pltpu.VMEM((2, n_node + 1, asked, half), BF),
            pltpu.VMEM((2, n_node + 1, asked, half), BF),
            pltpu.VMEM((chips, block, width), F32),
            pltpu.VMEM((2, chips, block, half), BF),
            pltpu.VMEM((2, chips, block, half), BF),
            dma((11,)),
            dma,
            dma,
            dma,
            dma,
            dma((n_node,)),
            dma((n_node,)),
            dma((n_node,)),
            dma((n_node,)),
            dma((2,)),
            dma((2,)),
            dma,
            dma,
            dma((2, n_node)),
            dma((2, n_node)),
            dma((2, n_node + 1)),
            dma((2, n_node + 1)),
            dma((2, chips)),
            dma((2, chips)),
        ],
        compiler_params=pltpu.CompilerParams(
            collective_id=0, has_side_effects=True, vmem_limit_bytes=60 * 1024 * 1024
        ),
        name="memory_step",
    )(
        ids,
        event_count,
        event_feat[0],
        requests[0][:, None, :],
        memory,
        w_input,
        w_state,
        w_pair,
        gate_bias.reshape(bias_rows, LANES),
        time_freq[None, :],
    )


def solution(mesh):
    by_device = ("node", "event")
    in_specs = (
        P("node", None),
        P(by_device, None, None, None),
        P(by_device, None, None),
        P(by_device, None, None),
        P(by_device, None, None),
        P(by_device, None, None),
        P(by_device, None),
        P(by_device, None, None),
        P(),
        P(),
        P(),
        P(),
        P(),
    )
    out_specs = P(by_device, None)
    return jax.shard_map(local, mesh=mesh, in_specs=in_specs, out_specs=out_specs, check_vma=False)
```

time: 46.6 us -> 38.4 us (0.82)
  local copies, waits for them, and re-layouts: 6.46 us -> 0.71 us
  Pallas kernels: 39.7 us -> 37.5 us
    unnamed x17 -> x1, local copies, waits for them, and re-layouts: 5.18 us -> 0.71 us
    pallas_call x1, Pallas kernels: 39.7 us -> 37.5 us  [local(): pl.pallas_call(functools.partial(kernel, n_node, n_event, chunk), out_sha...]
    concatenate x1 -> x0, local copies, waits for them, and re-layouts: 0.69 us -> none  [local(): packed = jnp.concatenate(parts, axis=1).reshape(shards, 1, LANES)]
    broadcast_in_dim x2 -> x0, local copies, waits for them, and re-layouts: 0.59 us -> none  [the longest x1 0.59 us: local(): gate_bias[None, :]]
where the time goes in v2:
time: 38.4 us; the launch traced here: 38.2 us
  Pallas kernels  37.5 us (98%)
  local copies, waits for them, and re-layouts  0.71 us (2%)
    pallas_call x1, Pallas kernels, local(): pl.pallas_call(functools.partial(kernel, n_node, n_event, chunk), out_sha...  37.5 us

profile of v2, /device:TPU:0, one launch (start us, length us, event | category | flops | bytes accessed | tf_op | source)
XLA Modules:
  0.0 38.2 jit_solution(6386166075011290189)
XLA Ops:
  0.0 37.5 %memory_step.1 = f32[256,256]{1,0:T(8,128)S(1)} custom-call(s32[16,32]{1,0:T(8,128)} %bitcast.17, s32[16,32]{1,0:T(8,128)} %bitcast.18, s32[16,32]{1,0:T(8,128)} %bitcast.19, s32[16,32]{1,0:T(8,128)} %bitcast.20, s32[1,32]{1,0:T(1,128)} %count_hbm.1, bf16[32,16,128]{2,1,0:T(8,128)(2,1)} %bitcast.16, s32[4,1,128]{2,1,0:T(1,128)} %bitcast.22, ...), custom_call_target="tpu_custom_call" | custom-call | tf_op jit(solution)/shard_map/memory_step/pallas_call | solution.py:512
  37.5 0.7 %copy.15 = f32[256,256]{1,0:T(8,128)} copy(f32[256,256]{1,0:T(8,128)S(1)} %memory_step.1) | data formatting | bytes 524288

commit v3 on v2

--- a/solution.py
+++ b/solution.py
@@ -42,6 +42,22 @@
 def spread_matrix(row, total, base):
     ids = lax.broadcasted_iota(jnp.int32, (total, row.shape[1]), 0) + base
     return one_hot(ids == row)
+
+
+def sigmoid(value):
+    return 0.5 * jnp.tanh(0.5 * value) + 0.5
+
+
+def cosine(value):
+    turns = jnp.floor(value * (1.0 / math.pi) + 0.5)
+    rest = (value - turns * 3.140625) - turns * (math.pi - 3.140625)
+    square = rest * rest
+    series = jnp.full_like(value, 1.0 / math.factorial(12))
+    for power in range(10, -1, -2):
+        sign = 1.0 if power % 4 == 0 else -1.0
+        series = series * square + sign / math.factorial(power)
+    odd = turns - 2.0 * jnp.floor(0.5 * turns)
+    return series * (1.0 - 2.0 * odd)
 
 
 def kernel(
@@ -69,6 +85,8 @@
     count,
     stage,
     pack,
+    feats_relay,
+    packs_relay,
     feats,
     packs,
     wanted,
@@ -84,6 +102,7 @@
     live,
     pick,
     spread,
+    place_own,
     place,
     table_grad,
     renew_grad,
@@ -101,6 +120,10 @@
     feat_recv,
     pack_send,
     pack_recv,
+    feat_out,
+    feat_in,
+    pack_out,
+    pack_in,
     req_send,
     req_recv,
     tab_send,
@@ -118,7 +141,6 @@
 ):
     shards = n_node * n_event
     node, event = lax.axis_index("node"), lax.axis_index("event")
-    me = node * n_event + event
     slots = feat_ref.shape[1]
     width = mem.shape[1]
     group_rows = mem.shape[0]
@@ -134,12 +156,18 @@
 
     barrier = pltpu.get_barrier_semaphore()
 
-    @pl.loop(1, shards)
+    def to_node(k):
+        return lax.rem(node + k, n_node)
+
+    def to_event(k):
+        return lax.rem(event + k, n_event)
+
+    for k in range(1, n_node):
+        pl.semaphore_signal(barrier, inc=1, device_id=(to_node(k), event), device_id_type=MESH)
+
+    @pl.loop(1, n_event)
     def _(k):
-        peer = lax.rem(me + k, shards)
-        pl.semaphore_signal(
-            barrier, inc=1, device_id=(peer // n_event, peer % n_event), device_id_type=MESH
-        )
+        pl.semaphore_signal(barrier, inc=1, device_id=(node, to_event(k)), device_id_type=MESH)
 
     small = [
         pltpu.make_async_copy(ids_hbm[k], ids.at[k], load_sem.at[k]) for k in range(4)
@@ -158,7 +186,9 @@
         )
     ]
     own_list = pltpu.make_async_copy(req_ref.at[node], wanted.at[node], req_recv.at[node])
-    own_feat = pltpu.make_async_copy(feat_ref.at[me], feats.at[me], feat_recv)
+    own_feat = pltpu.make_async_copy(
+        feat_ref.at[pl.ds(node * n_event, n_event)], feats_relay.at[node], feat_recv.at[node]
+    )
     for load in small + loads + [own_list, own_feat]:
         load.start()
     stage[...] = jnp.zeros_like(stage)
@@ -169,11 +199,8 @@
     slot = lax.broadcasted_iota(jnp.int32, (slots, shards), 0)
     stage[4 * slots : 5 * slots, :shards] = jnp.where(slot < count[...], 1, 0)
     pack[...] = stage[...].T[:shards].reshape(shards, 1, LANES)
-    packs[me] = pack[me]
-    pl.semaphore_wait(barrier, shards - 1)
-
-    def to_node(k):
-        return lax.rem(node + k, n_node)
+    packs_relay[node] = pack[pl.ds(node * n_event, n_event)]
+    pl.semaphore_wait(barrier, n_node + n_event - 2)
 
     def arrived(buffer, sem, slot):
         pltpu.make_async_copy(buffer.at[slot], buffer.at[slot], sem.at[slot]).wait()
@@ -192,26 +219,26 @@
     for k in range(n_node - 1, 0, -1):
         request_copy(k).start()
 
-    @pl.loop(1, shards)
-    def _(k):
-        peer = lax.rem(me + k, shards)
-        target = (peer // n_event, peer % n_event)
-        pltpu.make_async_remote_copy(
-            src_ref=pack.at[peer],
-            dst_ref=packs.at[me],
-            send_sem=pack_send,
-            recv_sem=pack_recv,
-            device_id=target,
+    def to_group(k, source, target, send_sem, recv_sem):
+        peer = to_node(k)
+        return pltpu.make_async_remote_copy(
+            src_ref=source.at[pl.ds(peer * n_event, n_event)],
+            dst_ref=target.at[node],
+            send_sem=send_sem.at[peer],
+            recv_sem=recv_sem.at[node],
+            device_id=(peer, event),
             device_id_type=MESH,
-        ).start()
-        pltpu.make_async_remote_copy(
-            src_ref=feat_ref.at[peer],
-            dst_ref=feats.at[me],
-            send_sem=feat_send,
-            recv_sem=feat_recv,
-            device_id=target,
-            device_id_type=MESH,
-        ).start()
+        )
+
+    def group_copies(k):
+        return (
+            to_group(k, pack, packs_relay, pack_send, pack_recv),
+            to_group(k, feat_ref, feats_relay, feat_send, feat_recv),
+        )
+
+    for k in range(n_node - 1, 0, -1):
+        for copy in group_copies(k):
+            copy.start()
 
     for k in range(n_node):
         arrived(wanted, req_recv, to_node(k))
@@ -248,11 +275,48 @@
     wanted_copy = to_sibling(wanted, wanted_pair, list_send.at[0], list_recv.at[0])
     wanted_copy.start()
 
-    pltpu.make_async_copy(feats, feats, feat_recv).wait()
-    others = packs.at[pl.ds(0, shards - 1)]
-    pltpu.make_async_copy(others, others, pack_recv).wait()
+    def to_owner(k, source, target, send_sem, recv_sem):
+        peer = to_event(k)
+        return pltpu.make_async_remote_copy(
+            src_ref=source.at[:, peer],
+            dst_ref=target.at[:, event],
+            send_sem=send_sem.at[peer],
+            recv_sem=recv_sem.at[event],
+            device_id=(node, peer),
+            device_id_type=MESH,
+        )
+
+    def owner_copies(k):
+        return (
+            to_owner(k, packs_relay, packs, pack_out, pack_in),
+            to_owner(k, feats_relay, feats, feat_out, feat_in),
+        )
+
+    for k in range(n_node):
+        if k > 0:
+            arrived(packs_relay, pack_recv, to_node(k))
+        arrived(feats_relay, feat_recv, to_node(k))
+
+    @pl.loop(1, n_event)
+    def _(k):
+        for copy in owner_copies(k):
+            copy.start()
+
+    kept = [
+        pltpu.make_async_copy(packs_relay.at[:, event], packs.at[:, event], pack_in.at[event]),
+        pltpu.make_async_copy(feats_relay.at[:, event], feats.at[:, event], feat_in.at[event]),
+    ]
+    for copy in kept:
+        copy.start()
+
     for load in loads[1:]:
         load.wait()
+
+    @pl.loop(0, n_event)
+    def _(e):
+        for buffer, sem in ((packs, pack_in), (feats, feat_in)):
+            pltpu.make_async_copy(buffer.at[:, e], buffer.at[:, e], sem.at[e]).wait()
+
     codes = packs[...].reshape(shards, LANES)
     code_parts = jnp.concatenate([codes >> 8, codes & 255], axis=1).astype(F32).astype(BF)
     kinds = 5
@@ -281,8 +345,9 @@
         source = columns[:, :LANES].astype(jnp.int32)
         current = mm(pick_matrix(source, group_rows), mem[...]).astype(BF)
         from_state = mm(current, wst[...])
-        timing = jnp.cos(times * freq[...]).astype(BF)
-        feature = feats[pl.ds(first, chunk // slots)].reshape(chunk, feat_ref.shape[2])
+        timing = cosine(times * freq[...]).astype(BF)
+        groups = chunk // (slots * n_event)
+        feature = feats[pl.ds(t * groups, groups)].reshape(chunk, feat_ref.shape[2])
         from_rest = mm(jnp.concatenate([feature, timing], axis=1), win[width:, :])
         prev[t] = current
         recur[t] = from_state[:, 2 * width :]
@@ -299,17 +364,18 @@
     source_copy.start()
     arrived_pair = pltpu.make_async_copy(wanted_pair, wanted_pair, list_recv.at[0])
     arrived_pair.wait()
+    listed_own = jnp.concatenate([wanted[node]] * 2 + [wanted_pair[node]] * 2, axis=1)
     listed = jnp.concatenate(
-        [wanted[g] for g in range(n_node)]
-        + [wanted[node]]
-        + [wanted_pair[g] for g in range(n_node)]
-        + [wanted_pair[node]],
+        [wanted[to_node(k)] for k in range(1, n_node)]
+        + [wanted_pair[to_node(k)] for k in range(1, n_node)],
         axis=1,
     )
 
     @pl.loop(0, chips)
     def _(j):
-        place[j] = spread_matrix(listed, block, (2 * j + core) * block)
+        base = (2 * j + core) * block
+        place_own[j] = spread_matrix(listed_own, block, base)
+        place[j] = spread_matrix(listed, block, base)
 
     for k in range(1, n_node):
         arrived(table, tab_recv, to_node(k))
@@ -324,8 +390,8 @@
         all_pre = pre[t] + mm(partner, win[:width, :])
         recurrent = recur[t]
         previous = prev[t].astype(F32)
-        reset = jax.nn.sigmoid(all_pre[:, :width])
-        update = jax.nn.sigmoid(all_pre[:, width : 2 * width])
+        reset = sigmoid(all_pre[:, :width])
+        update = sigmoid(all_pre[:, width : 2 * width])
         candidate = jnp.tanh(all_pre[:, 2 * width :] + reset * recurrent)
         renewed = (1.0 - update) * candidate + update * previous
         keys = mm(rows, wpair[...])
@@ -403,12 +469,23 @@
             total += mm(at, cur[t, 0]) + mm(at, cur[t, 1])
         acc[j] = total
 
+    for h in range(2):
+        arrived(back_pair.at[h], pass_recv.at[h], node)
+        arrived(back_pair.at[h], pass_recv.at[h], n_node)
+    own_rows = jnp.concatenate(
+        [
+            jnp.concatenate([held[0, at], held[1, at]], axis=1)
+            for held in (back_in, back_pair)
+            for at in (node, n_node)
+        ],
+        axis=0,
+    )
     pltpu.make_async_copy(source_pair, source_pair, list_recv.at[1]).wait()
     pltpu.make_async_copy(cur_pair, cur_pair, cur_recv).wait()
 
     @pl.loop(0, chips)
     def _(j):
-        total = acc[j]
+        total = acc[j] + mm(place_own[j], own_rows)
         for t in range(turns):
             at = spread_matrix(source_pair[t][:1], block, (2 * j + core) * block)
             total += mm(at, cur_pair[t, 0]) + mm(at, cur_pair[t, 1])
@@ -430,11 +507,11 @@
             slot = to_node(k)
             arrived(back_in.at[h], back_recv.at[h], slot)
             pass_copy(h, slot).start()
-        for slot in range(n_node + 1):
-            arrived(back_pair.at[h], pass_recv.at[h], slot)
-        rows = (n_node + 1) * asked
+        for k in range(1, n_node):
+            arrived(back_pair.at[h], pass_recv.at[h], to_node(k))
         returned = jnp.concatenate(
-            [back_in[h].reshape(rows, half), back_pair[h].reshape(rows, half)], axis=0
+            [held[h, to_node(k)] for held in (back_in, back_pair) for k in range(1, n_node)],
+            axis=0,
         )
 
         def whole_block(j):
@@ -469,9 +546,14 @@
     wanted_copy.wait_send()
     source_copy.wait_send()
     cur_copy.wait_send()
-    sent = feats.at[pl.ds(0, shards - 1)]
-    pltpu.make_async_copy(sent, sent, feat_send).wait()
-    pltpu.make_async_copy(others, others, pack_send).wait()
+    for k in range(1, n_node):
+        for copy in group_copies(k):
+            copy.wait_send()
+
+    @pl.loop(1, n_event)
+    def _(k):
+        for copy in owner_copies(k):
+            copy.wait_send()
 
 
 def local(
@@ -502,7 +584,7 @@
     chips = n_event // 2
     block = group_rows // n_event
     half = width // 2
-    listed = (n_node + 1) * asked
+    listed = (n_node - 1) * asked
     bias_rows = gate_bias.shape[0] // LANES
 
     vmem = pl.BlockSpec(memory_space=pltpu.VMEM)
@@ -525,8 +607,10 @@
             pltpu.VMEM((1, shards), jnp.int32),
             pltpu.VMEM((LANES, max(shards, LANES)), jnp.int32),
             pltpu.VMEM((shards, 1, LANES), jnp.int32),
-            pltpu.VMEM((shards, slots, feat_width), BF),
-            pltpu.VMEM((shards, 1, LANES), jnp.int32),
+            pltpu.VMEM((n_node, n_event, slots, feat_width), BF),
+            pltpu.VMEM((n_node, n_event, 1, LANES), jnp.int32),
+            pltpu.VMEM((n_node, n_event, slots, feat_width), BF),
+            pltpu.VMEM((n_node, n_event, 1, LANES), jnp.int32),
             pltpu.VMEM((n_node, 1, asked), jnp.int32),
             pltpu.VMEM((n_node, 1, asked), jnp.int32),
             pltpu.VMEM((n_node, asked, width), BF),
@@ -540,6 +624,7 @@
             pltpu.VMEM((turns, chunk, LANES), F32),
             pltpu.VMEM((turns, 2 * chunk, table_rows), BF),
             pltpu.VMEM((turns, table_rows, 2 * chunk), BF),
+            pltpu.VMEM((chips, block, 4 * asked), BF),
             pltpu.VMEM((chips, block, 2 * listed), BF),
             pltpu.VMEM((table_rows, width), F32),
             pltpu.VMEM((turns, chunk, width), F32),
@@ -553,10 +638,14 @@
             pltpu.VMEM((2, chips, block, half), BF),
             pltpu.VMEM((2, chips, block, half), BF),
             dma((11,)),
-            dma,
-            dma,
-            dma,
-            dma,
+            dma((n_node,)),
+            dma((n_node,)),
+            dma((n_node,)),
+            dma((n_node,)),
+            dma((n_event,)),
+            dma((n_event,)),
+            dma((n_event,)),
+            dma((n_event,)),
             dma((n_node,)),
             dma((n_node,)),
             dma((n_node,)),

time: 38.4 us -> 37.5 us (0.977)
  Pallas kernels: 37.5 us -> 36.6 us
    pallas_call x1, Pallas kernels: 37.5 us -> 36.6 us  [local(): pl.pallas_call(functools.partial(kernel, n_node, n_event, chunk), out_sha...]
where the time goes in v3:
time: 37.5 us; the launch traced here: 37.3 us
  Pallas kernels  36.6 us (98%)
  local copies, waits for them, and re-layouts  0.71 us (2%)
    pallas_call x1, Pallas kernels, local(): pl.pallas_call(functools.partial(kernel, n_node, n_event, chunk), out_sha...  36.6 us

profile of v3, /device:TPU:0, one launch (start us, length us, event | category | flops | bytes accessed | tf_op | source)
XLA Modules:
  0.0 37.3 jit_solution(3633524772591364112)
XLA Ops:
  0.0 36.6 %memory_step.1 = f32[256,256]{1,0:T(8,128)S(1)} custom-call(s32[16,32]{1,0:T(8,128)} %bitcast.17, s32[16,32]{1,0:T(8,128)} %bitcast.18, s32[16,32]{1,0:T(8,128)} %bitcast.19, s32[16,32]{1,0:T(8,128)} %bitcast.20, s32[1,32]{1,0:T(1,128)} %count_hbm.1, bf16[32,16,128]{2,1,0:T(8,128)(2,1)} %bitcast.16, s32[4,1,128]{2,1,0:T(1,128)} %bitcast.22, ...), custom_call_target="tpu_custom_call" | custom-call | tf_op jit(solution)/shard_map/memory_step/pallas_call | solution.py:594
  36.6 0.7 %copy.15 = f32[256,256]{1,0:T(8,128)} copy(f32[256,256]{1,0:T(8,128)S(1)} %memory_step.1) | data formatting | bytes 524288

commit v4 on v3

--- a/solution.py
+++ b/solution.py
@@ -191,6 +191,44 @@
     )
     for load in small + loads + [own_list, own_feat]:
         load.start()
+    pl.semaphore_wait(barrier, n_node + n_event - 2)
+
+    def arrived(buffer, sem, slot):
+        pltpu.make_async_copy(buffer.at[slot], buffer.at[slot], sem.at[slot]).wait()
+
+    def request_copy(k):
+        peer = to_node(k)
+        return pltpu.make_async_remote_copy(
+            src_ref=req_ref.at[peer],
+            dst_ref=wanted.at[node],
+            send_sem=req_send.at[peer],
+            recv_sem=req_recv.at[node],
+            device_id=(peer, event),
+            device_id_type=MESH,
+        )
+
+    for k in range(n_node - 1, 0, -1):
+        request_copy(k).start()
+
+    def to_group(k, source, target, send_sem, recv_sem):
+        peer = to_node(k)
+        return pltpu.make_async_remote_copy(
+            src_ref=source.at[pl.ds(peer * n_event, n_event)],
+            dst_ref=target.at[node],
+            send_sem=send_sem.at[peer],
+            recv_sem=recv_sem.at[node],
+            device_id=(peer, event),
+            device_id_type=MESH,
+        )
+
+    def group_copies(k):
+        return (
+            to_group(k, pack, packs_relay, pack_send, pack_recv),
+            to_group(k, feat_ref, feats_relay, feat_send, feat_recv),
+        )
+
+    for k in range(n_node - 1, 0, -1):
+        group_copies(k)[1].start()
     stage[...] = jnp.zeros_like(stage)
     for load in small:
         load.wait()
@@ -200,52 +238,8 @@
     stage[4 * slots : 5 * slots, :shards] = jnp.where(slot < count[...], 1, 0)
     pack[...] = stage[...].T[:shards].reshape(shards, 1, LANES)
     packs_relay[node] = pack[pl.ds(node * n_event, n_event)]
-    pl.semaphore_wait(barrier, n_node + n_event - 2)
-
-    def arrived(buffer, sem, slot):
-        pltpu.make_async_copy(buffer.at[slot], buffer.at[slot], sem.at[slot]).wait()
-
-    def request_copy(k):
-        peer = to_node(k)
-        return pltpu.make_async_remote_copy(
-            src_ref=req_ref.at[peer],
-            dst_ref=wanted.at[node],
-            send_sem=req_send.at[peer],
-            recv_sem=req_recv.at[node],
-            device_id=(peer, event),
-            device_id_type=MESH,
-        )
-
     for k in range(n_node - 1, 0, -1):
-        request_copy(k).start()
-
-    def to_group(k, source, target, send_sem, recv_sem):
-        peer = to_node(k)
-        return pltpu.make_async_remote_copy(
-            src_ref=source.at[pl.ds(peer * n_event, n_event)],
-            dst_ref=target.at[node],
-            send_sem=send_sem.at[peer],
-            recv_sem=recv_sem.at[node],
-            device_id=(peer, event),
-            device_id_type=MESH,
-        )
-
-    def group_copies(k):
-        return (
-            to_group(k, pack, packs_relay, pack_send, pack_recv),
-            to_group(k, feat_ref, feats_relay, feat_send, feat_recv),
-        )
-
-    for k in range(n_node - 1, 0, -1):
-        for copy in group_copies(k):
-            copy.start()
-
-    for k in range(n_node):
-        arrived(wanted, req_recv, to_node(k))
-    loads[0].wait()
-    columns = [jnp.broadcast_to(wanted[g], (LANES, asked)).T for g in range(n_node)]
-    picked = mm(pick_matrix(jnp.concatenate(columns, axis=0), group_rows), mem[...]).astype(BF)
-    fetched[...] = picked.reshape(n_node, asked, width)
+        group_copies(k)[0].start()
 
     def table_copy(k):
         peer = to_node(k)
@@ -258,9 +252,17 @@
             device_id_type=MESH,
         )
 
+    def fetch(k):
+        asker = to_node(k)
+        arrived(wanted, req_recv, asker)
+        column = jnp.broadcast_to(wanted[asker], (LANES, asked)).T
+        return mm(pick_matrix(column, group_rows), mem[...]).astype(BF)
+
+    loads[0].wait()
     for k in range(n_node - 1, 0, -1):
+        fetched[to_node(k)] = fetch(k)
         table_copy(k).start()
-    table[node] = fetched[node]
+    table[node] = fetch(0)
 
     def to_sibling(source, target, send_sem, recv_sem):
         return pltpu.make_async_remote_copy(
@@ -362,21 +364,6 @@
 
     source_copy = to_sibling(source_row, source_pair, list_send.at[1], list_recv.at[1])
     source_copy.start()
-    arrived_pair = pltpu.make_async_copy(wanted_pair, wanted_pair, list_recv.at[0])
-    arrived_pair.wait()
-    listed_own = jnp.concatenate([wanted[node]] * 2 + [wanted_pair[node]] * 2, axis=1)
-    listed = jnp.concatenate(
-        [wanted[to_node(k)] for k in range(1, n_node)]
-        + [wanted_pair[to_node(k)] for k in range(1, n_node)],
-        axis=1,
-    )
-
-    @pl.loop(0, chips)
-    def _(j):
-        base = (2 * j + core) * block
-        place_own[j] = spread_matrix(listed_own, block, base)
-        place[j] = spread_matrix(listed, block, base)
-
     for k in range(1, n_node):
         arrived(table, tab_recv, to_node(k))
     table_grad[...] = jnp.zeros_like(table_grad)
@@ -460,6 +447,20 @@
 
     cur_copy = to_sibling(cur, cur_pair, cur_send, cur_recv)
     cur_copy.start()
+    arrived_pair = pltpu.make_async_copy(wanted_pair, wanted_pair, list_recv.at[0])
+    arrived_pair.wait()
+    listed_own = jnp.concatenate([wanted[node]] * 2 + [wanted_pair[node]] * 2, axis=1)
+    listed = jnp.concatenate(
+        [wanted[to_node(k)] for k in range(1, n_node)]
+        + [wanted_pair[to_node(k)] for k in range(1, n_node)],
+        axis=1,
+    )
+
+    @pl.loop(0, chips)
+    def _(j):
+        base = (2 * j + core) * block
+        place_own[j] = spread_matrix(listed_own, block, base)
+        place[j] = spread_matrix(listed, block, base)
 
     @pl.loop(0, chips)
     def _(j):

time: 37.5 us -> 38.1 us (1.016)
  Pallas kernels: 36.6 us -> 37.2 us
    pallas_call x1, Pallas kernels: 36.6 us -> 37.2 us  [local(): pl.pallas_call(functools.partial(kernel, n_node, n_event, chunk), out_sha...]
where the time goes in v4:
time: 38.1 us; the launch traced here: 38 us
  Pallas kernels  37.2 us (98%)
  local copies, waits for them, and re-layouts  0.71 us (2%)
    pallas_call x1, Pallas kernels, local(): pl.pallas_call(functools.partial(kernel, n_node, n_event, chunk), out_sha...  37.2 us

profile of v4, /device:TPU:0, one launch (start us, length us, event | category | flops | bytes accessed | tf_op | source)
XLA Modules:
  0.0 38.0 jit_solution(11965578280508509680)
XLA Ops:
  0.0 37.2 %memory_step.1 = f32[256,256]{1,0:T(8,128)S(1)} custom-call(s32[16,32]{1,0:T(8,128)} %bitcast.17, s32[16,32]{1,0:T(8,128)} %bitcast.18, s32[16,32]{1,0:T(8,128)} %bitcast.19, s32[16,32]{1,0:T(8,128)} %bitcast.20, s32[1,32]{1,0:T(1,128)} %count_hbm.1, bf16[32,16,128]{2,1,0:T(8,128)(2,1)} %bitcast.16, s32[4,1,128]{2,1,0:T(1,128)} %bitcast.22, ...), custom_call_target="tpu_custom_call" | custom-call | tf_op jit(solution)/shard_map/memory_step/pallas_call | solution.py:595
  37.3 0.7 %copy.15 = f32[256,256]{1,0:T(8,128)} copy(f32[256,256]{1,0:T(8,128)S(1)} %memory_step.1) | data formatting | bytes 524288

commit v5 on v4

--- a/solution.py
+++ b/solution.py
@@ -58,6 +58,12 @@
         series = series * square + sign / math.factorial(power)
     odd = turns - 2.0 * jnp.floor(0.5 * turns)
     return series * (1.0 - 2.0 * odd)
+
+
+def each_turn(turns):
+    if turns == 1:
+        return lambda body: body(0)
+    return pl.loop(0, turns)
 
 
 def kernel(
@@ -84,6 +90,8 @@
     ids,
     count,
     stage,
+    gather_kind,
+    same_slot,
     pack,
     feats_relay,
     packs_relay,
@@ -191,6 +199,16 @@
     )
     for load in small + loads + [own_list, own_feat]:
         load.start()
+    slot_bits = slots.bit_length() - 1
+    kinds = 5
+    from_lane = lax.broadcasted_iota(jnp.int32, (2 * LANES, kinds * LANES), 0)
+    to_kind = lax.broadcasted_iota(jnp.int32, (2 * LANES, kinds * LANES), 1) >> 7
+    weight = jnp.where(from_lane < LANES, 256.0, 1.0)
+    same_kind = (from_lane & (LANES - 1)) >> slot_bits == to_kind
+    gather_kind[...] = jnp.where(same_kind, weight, 0.0).astype(BF)
+    lane = lax.broadcasted_iota(jnp.int32, (chunk, 2 * LANES), 1)
+    row = lax.broadcasted_iota(jnp.int32, (chunk, 2 * LANES), 0)
+    same_slot[...] = jnp.where(((lane ^ row) & (slots - 1)) == 0, 1.0, 0.0)
     pl.semaphore_wait(barrier, n_node + n_event - 2)
 
     def arrived(buffer, sem, slot):
@@ -252,17 +270,15 @@
             device_id_type=MESH,
         )
 
-    def fetch(k):
-        asker = to_node(k)
-        arrived(wanted, req_recv, asker)
-        column = jnp.broadcast_to(wanted[asker], (LANES, asked)).T
-        return mm(pick_matrix(column, group_rows), mem[...]).astype(BF)
-
+    for k in range(n_node):
+        arrived(wanted, req_recv, to_node(k))
+    columns = [jnp.broadcast_to(wanted[g], (LANES, asked)).T for g in range(n_node)]
     loads[0].wait()
+    picked = mm(pick_matrix(jnp.concatenate(columns, axis=0), group_rows), mem[...]).astype(BF)
+    fetched[...] = picked.reshape(n_node, asked, width)
     for k in range(n_node - 1, 0, -1):
-        fetched[to_node(k)] = fetch(k)
         table_copy(k).start()
-    table[node] = fetch(0)
+    table[node] = fetched[node]
 
     def to_sibling(source, target, send_sem, recv_sem):
         return pltpu.make_async_remote_copy(
@@ -321,23 +337,15 @@
 
     codes = packs[...].reshape(shards, LANES)
     code_parts = jnp.concatenate([codes >> 8, codes & 255], axis=1).astype(F32).astype(BF)
-    kinds = 5
-    from_lane = lax.broadcasted_iota(jnp.int32, (2 * LANES, kinds * LANES), 0)
-    to_kind = lax.broadcasted_iota(jnp.int32, (2 * LANES, kinds * LANES), 1) // LANES
-    weight = jnp.where(from_lane < LANES, 256.0, 1.0)
-    gather_kind = jnp.where((from_lane % LANES) // slots == to_kind, weight, 0.0).astype(BF)
     bias_row = jnp.concatenate([bias[k : k + 1, :] for k in range(bias.shape[0])], axis=1)
 
-    @pl.loop(0, turns)
+    @each_turn(turns)
     def _(t):
         first = t * (chunk // slots)
-        home = lax.broadcasted_iota(jnp.int32, (chunk, shards), 0) // slots + first
+        home = (lax.broadcasted_iota(jnp.int32, (chunk, shards), 0) >> slot_bits) + first
         from_home = one_hot(home == lax.broadcasted_iota(jnp.int32, (chunk, shards), 1))
-        mine = mm(from_home, code_parts)
-        lane = lax.broadcasted_iota(jnp.int32, (chunk, 2 * LANES), 1)
-        row = lax.broadcasted_iota(jnp.int32, (chunk, 2 * LANES), 0)
-        mine = jnp.where(lane % slots == row % slots, mine, 0.0).astype(BF)
-        columns = mm(mine, gather_kind)
+        mine = (mm(from_home, code_parts) * same_slot[...]).astype(BF)
+        columns = mm(mine, gather_kind[...])
         times = columns[:, 3 * LANES : 4 * LANES]
         live[t] = columns[:, 4 * LANES :]
         for kind in range(2):
@@ -369,7 +377,7 @@
     table_grad[...] = jnp.zeros_like(table_grad)
     factor = 1.0 / math.sqrt(width)
 
-    @pl.loop(0, turns)
+    @each_turn(turns)
     def _(t):
         rows = mm(pick[t], table[...].reshape(table_rows, width)).astype(BF)
         partner = rows[:chunk]
@@ -439,7 +447,7 @@
         pass_copy(h, node).start()
         pass_copy(h, n_node).start()
 
-    @pl.loop(0, turns)
+    @each_turn(turns)
     def _(t):
         high, low = split(renew_grad[t] + mm_nt(state_grad[t], wst[...]))
         cur[t, 0] = high
@@ -607,6 +615,8 @@
             pltpu.VMEM((4, slots, shards), jnp.int32),
             pltpu.VMEM((1, shards), jnp.int32),
             pltpu.VMEM((LANES, max(shards, LANES)), jnp.int32),
+            pltpu.VMEM((2 * LANES, 5 * LANES), BF),
+            pltpu.VMEM((chunk, 2 * LANES), F32),
             pltpu.VMEM((shards, 1, LANES), jnp.int32),
             pltpu.VMEM((n_node, n_event, slots, feat_width), BF),
             pltpu.VMEM((n_node, n_event, 1, LANES), jnp.int32),

time: 38.1 us -> 36.9 us (0.969)
  Pallas kernels: 37.2 us -> 36.1 us
    pallas_call x1, Pallas kernels: 37.2 us -> 36.1 us  [local(): pl.pallas_call(functools.partial(kernel, n_node, n_event, chunk), out_sha...]
where the time goes in v5:
time: 36.9 us; the launch traced here: 36.8 us
  Pallas kernels  36.1 us (98%)
  local copies, waits for them, and re-layouts  0.71 us (2%)
    pallas_call x1, Pallas kernels, local(): pl.pallas_call(functools.partial(kernel, n_node, n_event, chunk), out_sha...  36.1 us

profile of v5, /device:TPU:0, one launch (start us, length us, event | category | flops | bytes accessed | tf_op | source)
XLA Modules:
  0.0 36.8 jit_solution(5224135104065422896)
XLA Ops:
  0.0 36.1 %memory_step.1 = f32[256,256]{1,0:T(8,128)S(1)} custom-call(s32[16,32]{1,0:T(8,128)} %bitcast.17, s32[16,32]{1,0:T(8,128)} %bitcast.18, s32[16,32]{1,0:T(8,128)} %bitcast.19, s32[16,32]{1,0:T(8,128)} %bitcast.20, s32[1,32]{1,0:T(1,128)} %count_hbm.1, bf16[32,16,128]{2,1,0:T(8,128)(2,1)} %bitcast.16, s32[4,1,128]{2,1,0:T(1,128)} %bitcast.22, ...), custom_call_target="tpu_custom_call" | custom-call | tf_op jit(solution)/shard_map/memory_step/pallas_call | solution.py:603
  36.1 0.7 %copy.15 = f32[256,256]{1,0:T(8,128)} copy(f32[256,256]{1,0:T(8,128)S(1)} %memory_step.1) | data formatting | bytes 524288

commit v6 on v5

--- a/solution.py
+++ b/solution.py
@@ -108,6 +108,7 @@
     source_row,
     source_pair,
     live,
+    timing,
     pick,
     spread,
     place_own,
@@ -245,8 +246,6 @@
             to_group(k, feat_ref, feats_relay, feat_send, feat_recv),
         )
 
-    for k in range(n_node - 1, 0, -1):
-        group_copies(k)[1].start()
     stage[...] = jnp.zeros_like(stage)
     for load in small:
         load.wait()
@@ -258,6 +257,8 @@
     packs_relay[node] = pack[pl.ds(node * n_event, n_event)]
     for k in range(n_node - 1, 0, -1):
         group_copies(k)[0].start()
+    for k in range(n_node - 1, 0, -1):
+        group_copies(k)[1].start()
 
     def table_copy(k):
         peer = to_node(k)
@@ -310,30 +311,33 @@
             to_owner(k, feats_relay, feats, feat_out, feat_in),
         )
 
-    for k in range(n_node):
-        if k > 0:
-            arrived(packs_relay, pack_recv, to_node(k))
-        arrived(feats_relay, feat_recv, to_node(k))
-
-    @pl.loop(1, n_event)
-    def _(k):
-        for copy in owner_copies(k):
-            copy.start()
-
     kept = [
         pltpu.make_async_copy(packs_relay.at[:, event], packs.at[:, event], pack_in.at[event]),
         pltpu.make_async_copy(feats_relay.at[:, event], feats.at[:, event], feat_in.at[event]),
     ]
-    for copy in kept:
-        copy.start()
+    for k in range(1, n_node):
+        arrived(packs_relay, pack_recv, to_node(k))
+
+    @pl.loop(1, n_event)
+    def _(k):
+        owner_copies(k)[0].start()
+
+    kept[0].start()
+    for k in range(n_node):
+        arrived(feats_relay, feat_recv, to_node(k))
+
+    @pl.loop(1, n_event)
+    def _(k):
+        owner_copies(k)[1].start()
+
+    kept[1].start()
 
     for load in loads[1:]:
         load.wait()
 
     @pl.loop(0, n_event)
     def _(e):
-        for buffer, sem in ((packs, pack_in), (feats, feat_in)):
-            pltpu.make_async_copy(buffer.at[:, e], buffer.at[:, e], sem.at[e]).wait()
+        pltpu.make_async_copy(packs.at[:, e], packs.at[:, e], pack_in.at[e]).wait()
 
     codes = packs[...].reshape(shards, LANES)
     code_parts = jnp.concatenate([codes >> 8, codes & 255], axis=1).astype(F32).astype(BF)
@@ -355,20 +359,27 @@
         source = columns[:, :LANES].astype(jnp.int32)
         current = mm(pick_matrix(source, group_rows), mem[...]).astype(BF)
         from_state = mm(current, wst[...])
-        timing = cosine(times * freq[...]).astype(BF)
-        groups = chunk // (slots * n_event)
-        feature = feats[pl.ds(t * groups, groups)].reshape(chunk, feat_ref.shape[2])
-        from_rest = mm(jnp.concatenate([feature, timing], axis=1), win[width:, :])
+        timing[t] = cosine(times * freq[...]).astype(BF)
         prev[t] = current
         recur[t] = from_state[:, 2 * width :]
-        gates = from_rest[:, : 2 * width] + from_state[:, : 2 * width]
-        pre[t] = jnp.concatenate([gates, from_rest[:, 2 * width :]], axis=1) + bias_row
+        gates = [from_state[:, : 2 * width], jnp.zeros((chunk, width), F32)]
+        pre[t] = jnp.concatenate(gates, axis=1) + bias_row
         for kind in range(2):
             column = columns[:, (kind + 1) * LANES : (kind + 2) * LANES].astype(jnp.int32)
             pick[t, kind * chunk : (kind + 1) * chunk] = pick_matrix(column, table_rows)
             spread[t, :, kind * chunk : (kind + 1) * chunk] = spread_matrix(
                 ids_row[t, kind][:1], table_rows, 0
             )
+
+    @pl.loop(0, n_event)
+    def _(e):
+        pltpu.make_async_copy(feats.at[:, e], feats.at[:, e], feat_in.at[e]).wait()
+
+    @each_turn(turns)
+    def _(t):
+        groups = chunk // (slots * n_event)
+        feature = feats[pl.ds(t * groups, groups)].reshape(chunk, feat_ref.shape[2])
+        pre[t] += mm(jnp.concatenate([feature, timing[t]], axis=1), win[width:, :])
 
     source_copy = to_sibling(source_row, source_pair, list_send.at[1], list_recv.at[1])
     source_copy.start()
@@ -633,6 +644,7 @@
             pltpu.VMEM((turns, 8, chunk), jnp.int32),
             pltpu.VMEM((turns, 8, chunk), jnp.int32),
             pltpu.VMEM((turns, chunk, LANES), F32),
+            pltpu.VMEM((turns, chunk, LANES), BF),
             pltpu.VMEM((turns, 2 * chunk, table_rows), BF),
             pltpu.VMEM((turns, table_rows, 2 * chunk), BF),
             pltpu.VMEM((chips, block, 4 * asked), BF),

time: 36.9 us -> 36.8 us (level)
  no operation moved by 1% of the time
where the time goes in v6:
time: 36.8 us; the launch traced here: 36.7 us
  Pallas kernels  36 us (98%)
  local copies, waits for them, and re-layouts  0.71 us (2%)
    pallas_call x1, Pallas kernels, local(): pl.pallas_call(functools.partial(kernel, n_node, n_event, chunk), out_sha...  36 us

profile of v6, /device:TPU:0, one launch (start us, length us, event | category | flops | bytes accessed | tf_op | source)
XLA Modules:
  0.0 36.7 jit_solution(2573726242332513874)
XLA Ops:
  0.0 36.0 %memory_step.1 = f32[256,256]{1,0:T(8,128)S(1)} custom-call(s32[16,32]{1,0:T(8,128)} %bitcast.17, s32[16,32]{1,0:T(8,128)} %bitcast.18, s32[16,32]{1,0:T(8,128)} %bitcast.19, s32[16,32]{1,0:T(8,128)} %bitcast.20, s32[1,32]{1,0:T(1,128)} %count_hbm.1, bf16[32,16,128]{2,1,0:T(8,128)(2,1)} %bitcast.16, s32[4,1,128]{2,1,0:T(1,128)} %bitcast.22, ...), custom_call_target="tpu_custom_call" | custom-call | tf_op jit(solution)/shard_map/memory_step/pallas_call | solution.py:614
  36.0 0.7 %copy.15 = f32[256,256]{1,0:T(8,128)} copy(f32[256,256]{1,0:T(8,128)S(1)} %memory_step.1) | data formatting | bytes 524288
